TPU v7x, 128 devices: a whole 4x4x4 slice. The times are simulated.
128 devices in a mesh: bx: 16 (over y_lo, z, core), by: 8 (over x, y_hi).
Axes of the slice: x: 4, y: 4 (y_hi: 2, y_lo: 2; y = y_hi * 2 + y_lo), z: 4, core: 2. Of those that a mesh axis runs over, the one named last changes fastest.
Arguments:
- charges: bfloat16 [262144, 128], P(('bx', 'by')), may hold values from -6 to 6
- weight_tiles: bfloat16 [32, 128, 512], replicated, may hold values from 0 to 0.14941406
- block_shape: int32 [262144], P(('bx', 'by')), may hold values from 0 to 31
- block_box: int32 [262144], P(('bx', 'by')), may hold values from 0 to 32767
- live_blocks: int32 [128], P(('bx', 'by')), may hold values from 1 to 2048, 131072 in all
Outputs:
- coarse: float32 [128, 2048, 512], P('bx', 'by')
Inputs may be any that keep to these rules, and one draw needn't show every extreme that they name: `live_blocks`: live slots of a device are its first ones; some device uses all 2048 slots.
All inputs are finite; a program needn't handle non-finite values.
Results may differ from a plain program's by a relative error of at most 0.0003.
Values may be sent and summed in bfloat16 or wider, within the bound.
No kernel may reach another device: no remote copies, remote signals or barrier semaphores. Data moves between devices by JAX's collectives and lax.ppermute only.
A program may use at most 192 MiB of HBM per device.

v0:
```python
import jax
import jax.numpy as jnp
from jax import lax
from jax.sharding import PartitionSpec as P

CX = 64
CY = 256
NZ = 128


def from_behind(block, axis, distance):
    devices = range(lax.axis_size(axis))
    route = [((i - distance) % len(devices), i) for i in devices]
    return lax.ppermute(block, axis, route)


def restrict_pencil(pencil):
    length = pencil.shape[0]
    half_len = length // 2
    extended = jnp.concatenate([pencil[length - 2 :], pencil, pencil[:2]], axis=0)
    paired = extended.reshape(half_len + 2, 2, pencil.shape[1], pencil.shape[2])
    even_rows = paired[:, 0]
    odd_rows = paired[:, 1]
    reduced = (
        even_rows[:half_len]
        + 4.0 * odd_rows[:half_len]
        + 6.0 * even_rows[1 : half_len + 1]
        + 4.0 * odd_rows[1 : half_len + 1]
        + even_rows[2 : half_len + 2]
    ) / 8.0
    return jnp.transpose(reduced, (2, 1, 0))


def products(block_q, block_s, wflat, count, group):
    total = block_q.shape[0]
    shapes_n = wflat.shape[0] // block_q.shape[1]
    atoms = block_q.shape[1]
    turns = (count + group - 1) // group

    def one_turn(step, acc):
        begin = step * group
        qg = lax.dynamic_slice_in_dim(block_q, begin, group, 0)
        sg = lax.dynamic_slice_in_dim(block_s, begin, group, 0)
        slot = begin + jnp.arange(group, dtype=jnp.int32)
        pick = (sg[:, None] == jnp.arange(shapes_n, dtype=jnp.int32)[None, :]) & (slot < count)[
            :, None
        ]
        spread = jnp.where(pick[:, :, None], qg[:, None, :], jnp.zeros((), qg.dtype)).reshape(
            group, shapes_n * atoms
        )
        part = jnp.dot(spread, wflat, preferred_element_type=jnp.float32)
        return lax.dynamic_update_slice_in_dim(acc, part, begin, 0)

    start = jnp.zeros((total, wflat.shape[1]), jnp.float32)
    return lax.fori_loop(0, turns, one_turn, start)


def deposit(tiles, block_box):
    ybox = CY // 4
    zbox = NZ // 4
    count = tiles.shape[0]
    ux = block_box // (ybox * zbox)
    vy = block_box // zbox % ybox
    wz = block_box % zbox
    columns = tiles.reshape(count, 64, 8)
    spot = (4 * wz[:, None] - 2 + jnp.arange(8, dtype=jnp.int32)[None, :]) % NZ
    lanes = jnp.arange(NZ, dtype=jnp.int32)
    placing = (spot[:, :, None] == lanes[None, None, :]).astype(jnp.float32)
    lines = jnp.einsum("bkr,brz->bkz", columns, placing, precision=lax.Precision.HIGHEST)
    plane = jnp.arange(64, dtype=jnp.int32)
    target = (
        (4 * ux[:, None] + plane[None, :] // 8) * (CY + 4) + 4 * vy[:, None] + plane[None, :] % 8
    ).reshape(-1)
    grid = (
        jnp.zeros(((CX + 4) * (CY + 4), NZ), jnp.float32)
        .at[target]
        .add(lines.reshape(count * 64, NZ))
    )
    return grid.reshape(CX + 4, CY + 4, NZ)


def fold_y(field):
    width = field.shape[1] - 4
    upper = field[:, width + 2 :]
    lower = field[:, :2]
    inner = field[:, 2 : width + 2]
    from_below = from_behind(upper, "by", 1)
    from_above = from_behind(lower, "by", -1)
    inner = inner.at[:, :2].add(from_below)
    inner = inner.at[:, width - 2 :].add(from_above)
    return inner


def on_device(charges, weight_tiles, block_shape, block_box, live_blocks):
    nblk, atoms = charges.shape
    shapes_n, _, cells = weight_tiles.shape
    wflat = weight_tiles.reshape(shapes_n * atoms, cells)
    half = nblk // 2
    group = min(256, half)
    live = live_blocks[0]
    tiles = products(charges, block_shape, wflat, live, group)
    padded = deposit(tiles, block_box)
    upper = padded[CX + 2 :]
    lower = padded[:2]
    inner = padded[2 : CX + 2]
    from_left = from_behind(upper, "bx", 1)
    from_right = from_behind(lower, "bx", -1)
    inner = inner.at[:2].add(from_left)
    inner = inner.at[CX - 2 :].add(from_right)
    summed = fold_y(inner)
    return restrict_pencil(lax.all_to_all(summed, "bx", split_axis=2, concat_axis=0, tiled=True))


def solution(mesh):
    return jax.shard_map(
        on_device,
        mesh=mesh,
        in_specs=(P(("bx", "by"), None), P(), P(("bx", "by")), P(("bx", "by")), P(("bx", "by"))),
        out_specs=P("bx", "by", None),
        check_vma=False,
    )
```

profile of v0, /device:TPU:0, one launch (start us, length us, event | category | flops | bytes accessed | tf_op | source)
XLA Modules:
  0.0 1019.3 jit_solution(5008191768540451328)
XLA Ops:
  0.7 2.5 broadcast_in_dim.30.clone
  3.2 73.6 %while.14 = (s32[]{:T(128)}, f32[2048,512]{0,1:T(8,128)}, s32[]{:T(128)}, s32[2048]{0:T(1024)}, s32[]{:T(128)}, /*index=5*/bf16[2048,128]{1,0:T(8,128)(2,1)}, bf...) while((s32[]{:T(128)}, f32[2048,512]{0,1:T(8,128)}, s32[]{:T(128)}, ...), condition=%wide.region_1.2_spmd, body=%wide.region_0.1_spmd.sunk | while | flops 1074807296 | bytes 9129647 | solution.py:55
  4.8 0.9 constant_dynamic-slice_fusion.2
  5.6 1.6 broadcast_select_fusion.2
  7.3 5.2 fusion.44
  14.0 0.9 constant_dynamic-slice_fusion.2
  14.8 1.6 broadcast_select_fusion.2
  16.5 5.2 fusion.44
  21.6 0.8 dynamic_slice.10
  23.2 0.9 constant_dynamic-slice_fusion.2
  24.0 1.6 broadcast_select_fusion.2
  25.7 5.2 fusion.44
  32.4 0.9 constant_dynamic-slice_fusion.2
  33.2 1.6 broadcast_select_fusion.2
  34.9 5.2 fusion.44
  41.6 0.9 constant_dynamic-slice_fusion.2
  42.4 1.6 broadcast_select_fusion.2
  44.1 5.2 fusion.44
  50.8 0.9 constant_dynamic-slice_fusion.2
  51.6 1.6 broadcast_select_fusion.2
  53.3 5.2 fusion.44
  60.0 0.9 constant_dynamic-slice_fusion.2
  60.8 1.6 broadcast_select_fusion.2
  62.5 5.2 fusion.44
  69.2 0.9 constant_dynamic-slice_fusion.2
  70.0 1.6 broadcast_select_fusion.2
  71.7 5.2 fusion.44
  76.8 7.5 copy.13
  86.7 63.5 %fusion.7 = f32[2048,64,128]{2,1,0:T(8,128)} fusion(f32[2048,64,8]{1,2,0:T(8,128)} %copy.13, s32[2048,8]{1,0:T(8,128)S(1)} %add_select_fusion), kind=kOutput, calls=%fused_computation.12 | convolution fusion | flops 1612709888 | bytes 71368704 | tf_op jit(solution)/shard_map/bkr,brz->bkz/dot_general | solution.py:69
  150.1 698.3 %scatter_custom_fusion = f32[17680,128]{1,0:T(8,128)} fusion(s32[131072]{0:T(1024)S(1)} %bitcast.36, f32[131072,128]{1,0:T(8,128)} %bitcast.4, f32[]{:T(128)} %constant.219.clone.1), kind=kCustom, calls=%fused_computation.13 | custom fusion | flops 16777216 | bytes 9052672 | tf_op jit(solution)/shard_map/scatter-add | solution.py:77
  848.5 1.2 fusion.31
  849.8 3.9 collective-permute-start.1
  853.7 7.7 slice.182
  861.4 9.1 slice.162
  871.3 1.7 fusion.20
  873.0 1.1 fusion.32
  874.1 3.3 collective-permute-start.2
  877.4 7.9 slice.187
  885.3 2.4 collective-permute-start.3
  887.7 1.6 fusion.22
  889.3 1.8 collective-permute-done.3
  891.1 1.6 fusion.21
  892.7 9.2 copy.14
  902.0 98.9 %all_to_all.18 = f32[64,256,128]{1,0,2:T(8,128)S(1)} all-to-all(f32[64,256,128]{1,0,2:T(8,128)} %copy.14), channel_id=1, replica_groups=mesh['bx'=16,'by'=8] {'bx'}, dimensions={2} | all-to-all | bytes 16777216 | tf_op jit(solution)/shard_map/all_to_all | solution.py:111
  1000.9 6.6 copy.16
  1007.5 2.6 pad_maximum_fusion
  1010.1 4.0 fusion.11
  1014.1 5.2 copy.17
  (40 shorter events, 14.8 us)
Async XLA Ops:
  76.8 7.5 copy-start
  849.7 20.9 %collective-permute-start = (f32[2,260,128]{2,1,0:T(8,128)S(1)}, f32[2,260,128]{2,1,0:T(8,128)S(1)}, u32[]{:S(2)}, u32[]{:S(2)}) collective-permute-start(f32[2,260,128]{2,1,0:T(8,128)S(1)} %slice.165), channel_id=1, source_target_pairs={{120,0},{0,8},{8,16},{16,24},{24,32},{32,40},{40,48},{48,56},{56,6... | collective-permute-start | bytes 798728 | tf_op jit(solution)/shard_map/ppermute | solution.py:14
  849.8 21.5 %collective-permute-start.1 = (f32[2,260,128]{2,1,0:T(8,128)S(1)}, f32[2,260,128]{2,1,0:T(8,128)S(1)}, u32[]{:S(2)}, u32[]{:S(2)}) collective-permute-start(f32[2,260,128]{2,1,0:T(8,128)S(1)} %slice.168), channel_id=1, source_target_pairs={{8,0},{16,8},{24,16},{32,24},{40,32},{48,40},{56,48},{64,56},{72,6... | collective-permute-start | bytes 798728 | tf_op jit(solution)/shard_map/ppermute | solution.py:14
  874.1 13.6 %collective-permute-start.2 = (f32[64,2,128]{2,1,0:T(2,128)S(1)}, f32[64,2,128]{2,1,0:T(2,128)S(1)}, u32[]{:S(2)}, u32[]{:S(2)}) collective-permute-start(f32[64,2,128]{2,1,0:T(2,128)S(1)} %get-tuple-element.110), channel_id=1, source_target_pairs={{7,0},{0,1},{1,2},{2,3},{3,4},{4,5},{5,6},{6,7},{15,8},{8,9},{9,10... | collective-permute-start | bytes 196616 | tf_op jit(solution)/shard_map/ppermute | solution.py:14
  885.3 5.8 collective-permute-start.3
where the time goes:
time: 1020 us
  other arithmetic  731 us (72%)
  matrix products  105 us (10%)
  blocking collectives  98.9 us (10%)
  local copies, waits for them, and re-layouts  71.7 us (7%)
    scatter-add x1, other arithmetic, deposit(): grid = jnp.zeros(((CX + 4) * (CY + 4), NZ), jnp.float32).at[target].add(l...  698 us
    all_to_all x1, blocking collectives, on_device(): lax.all_to_all(summed, 'bx', split_axis=2, concat_axis=0, tiled=True)  98.9 us
    dot_general x1, matrix products, deposit(): jnp.einsum('bkr,brz->bkz', columns, placing, precision=lax.Precision.HIGH...  63.5 us
    dynamic_update_slice x8, matrix products, one_turn(): return lax.dynamic_update_slice_in_dim(acc, part, begin, 0)  41.4 us
  transfers between devices with their start and end apart: 4, of which 1 were waited for; matrix products, arithmetic and copies ran while one was open for 3% of the time, Pallas kernels for 0%

commit v1 on v0

v1 whole, which is shorter than its diff:
```python
import jax
import jax.numpy as jnp
import numpy as np
from jax import lax
from jax.experimental import pallas as pl
from jax.experimental.pallas import tpu as pltpu
from jax.sharding import PartitionSpec as P

NZ = 128
GROUP = 256
BATCH = 16
KZ = 16
UROWS = 18
VSLOTS = 36
PLANE = UROWS * VSLOTS
GROWS = 4 * KZ * PLANE
SPARE = 256
VOUT = 34
TAIL = VOUT * 16
SENT = TAIL + 80
WIRE = jnp.int16
LEVELS = 32700.0
SCALE_ROW = TAIL + 34


def restriction():
    coef = [1.0, 4.0, 6.0, 4.0, 1.0]
    table = np.zeros((512, 384), np.float32)
    for p in range(8):
        for mm in range(6):
            tap = p + 4 - 2 * mm
            if not 0 <= tap < 5:
                continue
            for q in range(8):
                for r in range(8):
                    lane = (mm % 2) * 64 + ((r - 2) % 8) * 8 + (q - 2) % 8
                    table[(p * 8 + q) * 8 + r, (mm // 2) * 128 + lane] = coef[tap] / 8.0
    return table


def spread_kernel(base_ref, clash_ref, live_ref, q_ref, s_ref, w_ref, r_ref, out_ref, grid_ref, pick_ref, tile_ref, plane_ref):
    k = pl.program_id(0)
    shapes_n = w_ref.shape[0] // 128

    @pl.when(k == 0)
    def _():
        def clear(step, carry):
            grid_ref[pl.ds(pl.multiple_of(step * 256, 256), 256), :] = jnp.zeros((256, 128), jnp.float32)
            return carry

        lax.fori_loop(0, (GROWS + SPARE) // 256, clear, 0)

        def one_group(step, carry):
            begin = pl.multiple_of(step * GROUP, GROUP)
            qg = q_ref[pl.ds(begin, GROUP), :]
            sg = s_ref[pl.ds(begin, GROUP), :]
            for s in range(shapes_n):
                pick_ref[:, s * 128 : (s + 1) * 128] = jnp.where(sg == s, qg, jnp.zeros_like(qg))
            part = jnp.dot(pick_ref[...], w_ref[...], preferred_element_type=jnp.float32)
            high = part.astype(jnp.bfloat16)
            low = (part - high.astype(jnp.float32)).astype(jnp.bfloat16)
            cells = jnp.dot(high, r_ref[...], preferred_element_type=jnp.float32)
            cells = cells + jnp.dot(low, r_ref[...], preferred_element_type=jnp.float32)
            for du in range(3):
                tile_ref[pl.ds(du, GROUP, stride=4), :] = cells[:, du * 128 : (du + 1) * 128]

            def one_batch(batch, inner):
                first = begin + batch * BATCH
                clash = clash_ref[step * (GROUP // BATCH) + batch]
                rows = [base_ref[first + j] for j in range(BATCH)]
                at = [pl.multiple_of(batch * BATCH * 4, 8) + 4 * j for j in range(BATCH)]

                @pl.when(clash == 0)
                def _():
                    sums = [grid_ref[pl.ds(rows[j], 3), :] + tile_ref[pl.ds(at[j], 3), :] for j in range(BATCH)]
                    for j in range(BATCH):
                        grid_ref[pl.ds(rows[j], 3), :] = sums[j]

                @pl.when(clash != 0)
                def _():
                    for j in range(BATCH):
                        grid_ref[pl.ds(rows[j], 3), :] += tile_ref[pl.ds(at[j], 3), :]

                return inner

            return lax.fori_loop(0, GROUP // BATCH, one_batch, carry)

        lax.fori_loop(0, (live_ref[0] + GROUP - 1) // GROUP, one_group, 0)

    lane = lax.broadcasted_iota(jnp.int32, (8, 128), 1)
    zoff = lane // 8 % 8
    yoff = lane % 8
    next_k = lax.rem(k + 1, KZ)
    last_k = lax.rem(k + KZ - 1, KZ)

    def swap(value, bit):
        return jnp.where(lane // bit % 2 == 1, pltpu.roll(value, bit, 1), pltpu.roll(value, 128 - bit, 1))

    def combined(row, stride):
        def at(copy, plane, dv):
            start = (copy * KZ + plane) * PLANE + row + dv * UROWS
            if stride is None:
                return grid_ref[pl.ds(start, 8), :]
            return grid_ref[pl.ds(start, 8, stride=stride), :]

        def even(pv, dv):
            return jnp.where(zoff < 6, at(pv, k, dv), at(pv, next_k, dv))

        def odd(pv, dv):
            return jnp.where(zoff // 2 == 2, at(2 + pv, last_k, dv), at(2 + pv, k, dv))

        def along_y(get):
            straight = jnp.where(yoff < 6, get(0, 0), get(0, 1))
            crossed = jnp.where(yoff // 2 == 2, get(1, -1), get(1, 0))
            return straight + swap(crossed, 4)

        return along_y(even) + swap(along_y(odd), 32)

    def one_slab(v, top):
        row = (v + 1) * UROWS + 1
        begin = pl.multiple_of(v * 16, 16)
        for half in range(2):
            value = combined(row + 8 * half, None)
            plane_ref[pl.ds(begin + 8 * half, 8), :] = value
            top = jnp.maximum(top, jnp.abs(value))
        return top

    top = lax.fori_loop(0, VOUT, one_slab, jnp.zeros((8, 128), jnp.float32))
    line = lax.broadcasted_iota(jnp.int32, (8, 128), 0)
    for side in range(2):
        for c in range(5):
            value = combined((8 * c + 1) * UROWS + side * 17, UROWS)
            if c == 4:
                value = jnp.where(line < 2, value, 0.0)
            plane_ref[TAIL + side * 40 + c * 8 : TAIL + side * 40 + c * 8 + 8, :] = value
            top = jnp.maximum(top, jnp.abs(value))
    top = jnp.maximum(jnp.max(top, axis=0, keepdims=True), 1e-37)
    power = jnp.ceil(jnp.log2(top) * 16.0 + 0.01)
    shrink = jnp.exp2(power * -0.0625)
    last = plane_ref[SCALE_ROW - 2 : SCALE_ROW + 6, :]
    whole = jnp.round(plane_ref[...] * shrink * LEVELS)
    out_ref[0] = whole.astype(jnp.int32).astype(out_ref.dtype)
    marked = jnp.where(line == 2, power, jnp.round(last * shrink * LEVELS))
    both = jnp.concatenate([marked, jnp.round(plane_ref[SCALE_ROW + 6 : SCALE_ROW + 14, :] * shrink * LEVELS)], axis=0)
    out_ref[0, SCALE_ROW - 2 : SCALE_ROW + 14, :] = both.astype(jnp.int32).astype(out_ref.dtype)


def gather_kernel(x_ref, out_ref, edge_ref, tail_ref, turn_ref, grow_ref):
    step = pl.program_id(0)

    @pl.when(step == 0)
    def _():
        for src in range(16):
            tail = x_ref[src, TAIL:SENT, :].astype(jnp.float32)
            grow = jnp.exp2(tail[SCALE_ROW - TAIL : SCALE_ROW - TAIL + 1] * 0.0625) / LEVELS
            grow_ref[src * 8 : src * 8 + 8, :] = jnp.broadcast_to(grow, (8, 128))
            tail_ref[src * 80 : (src + 1) * 80, :] = tail * grow

    lane = lax.broadcasted_iota(jnp.int32, (8, 128), 1)
    line = lax.broadcasted_iota(jnp.int32, (8, 128), 0)
    first = jnp.where(step == 0, 0, 2 * step - 1)
    second = jnp.where(step == 0, VOUT - 1, 2 * step)
    for src in range(16):
        grow = grow_ref[src * 8 : src * 8 + 8, :]
        halves = []
        for v in (first, second):
            both = x_ref[src, pl.ds(pl.multiple_of(v * 16, 16), 16), :].astype(jnp.float32)
            above = tail_ref[pl.ds((src + 1) % 16 * 80 + v, 1), :]
            below = tail_ref[pl.ds((src + 15) % 16 * 80 + 40 + v, 1), :]
            upper = both[0:8] * grow + jnp.where(line == 0, below, 0.0)
            lower = both[8:16] * grow + jnp.where(line == 7, above, 0.0)
            halves.append((upper, lower))
        for half in range(2):
            da, db = halves[0][half], halves[1][half]
            begin = src * 32 + half * 16
            turn_ref[pl.ds(begin, 8, stride=2), :] = jnp.where(lane < 64, da, pltpu.roll(db, 64, 1))
            turn_ref[pl.ds(begin + 1, 8, stride=2), :] = jnp.where(lane < 64, pltpu.roll(da, 64, 1), db)

    def emit(store):
        for c in range(4):
            block = turn_ref[c * 128 : (c + 1) * 128, :].T.reshape(2, 8, 8, 128)
            store(c, block)

    @pl.when(step == 0)
    def _():
        def store(c, block):
            edge_ref[:, :, :, c * 128 : (c + 1) * 128] = block

        emit(store)

    @pl.when(step != 0)
    def _():
        def store(c, block):
            out_ref[:, 0:8, c * 128 : (c + 1) * 128] = block[0]
            out_ref[:, 8:16, c * 128 : (c + 1) * 128] = block[1]

        emit(store)


def from_behind(block, axis, distance):
    devices = range(lax.axis_size(axis))
    route = [((i - distance) % len(devices), i) for i in devices]
    return lax.ppermute(block, axis, route)


def on_device(charges, weight_tiles, block_shape, block_box, live_blocks):
    nblk, atoms = charges.shape
    shapes_n, _, cells = weight_tiles.shape
    wflat = weight_tiles.reshape(shapes_n * atoms, cells)
    slot = jnp.arange(nblk, dtype=jnp.int32)
    shape = jnp.where(slot < live_blocks[0], block_shape, shapes_n)
    shape = jnp.broadcast_to(shape.astype(jnp.bfloat16)[:, None], (nblk, 128))
    u = block_box // 2048
    v = block_box // 32 % 64
    w = block_box % 32
    copy = (w % 2) * 2 + v % 2
    base = (copy * KZ + w // 2) * PLANE + (v // 2 + 2) * UROWS + u
    batched = base.reshape(nblk // BATCH, BATCH).T
    near = jnp.abs(batched[:, None, :] - batched[None, :, :]) < 3
    order = np.arange(BATCH)[:, None] < np.arange(BATCH)[None, :]
    clash = jnp.any(near & order[:, :, None], axis=(0, 1)).astype(jnp.int32)

    whole = lambda shp: pl.BlockSpec(shp, lambda k, *_: (0,) * len(shp), pipeline_mode=pl.Buffered(1))
    sent = pl.pallas_call(
        spread_kernel,
        out_shape=jax.ShapeDtypeStruct((KZ, SENT, 128), WIRE),
        grid_spec=pltpu.PrefetchScalarGridSpec(
            num_scalar_prefetch=3,
            grid=(KZ,),
            in_specs=[whole((nblk, 128)), whole((nblk, 128)), whole((shapes_n * atoms, cells)), whole((512, 384))],
            out_specs=pl.BlockSpec((1, SENT, 128), lambda k, *_: (k, 0, 0)),
            scratch_shapes=[
                pltpu.VMEM((GROWS + SPARE, 128), jnp.float32),
                pltpu.VMEM((GROUP, shapes_n * atoms), jnp.bfloat16),
                pltpu.VMEM((GROUP * 4, 128), jnp.float32),
                pltpu.VMEM((SENT, 128), jnp.float32),
            ],
        ),
        compiler_params=pltpu.CompilerParams(vmem_limit_bytes=56 * 1024 * 1024),
        name="spread",
    )(base, clash, live_blocks, charges, shape, wflat, jnp.asarray(restriction(), jnp.bfloat16))
    got = lax.all_to_all(sent, "bx", split_axis=0, concat_axis=0, tiled=True)
    main, edge = pl.pallas_call(
        gather_kernel,
        out_shape=(
            jax.ShapeDtypeStruct((8, 256, 512), jnp.float32),
            jax.ShapeDtypeStruct((2, 8, 8, 512), jnp.float32),
        ),
        grid=(17,),
        in_specs=[pl.BlockSpec((KZ, SENT, 128), lambda p: (0, 0, 0), pipeline_mode=pl.Buffered(1))],
        out_specs=(
            pl.BlockSpec((8, 16, 512), lambda p: (0, jnp.maximum(p - 1, 0), 0)),
            pl.BlockSpec((2, 8, 8, 512), lambda p: (0, 0, 0, 0)),
        ),
        scratch_shapes=[pltpu.VMEM((16 * 80, 128), jnp.float32), pltpu.VMEM((512, 128), jnp.float32), pltpu.VMEM((128, 128), jnp.float32)],
        compiler_params=pltpu.CompilerParams(vmem_limit_bytes=40 * 1024 * 1024),
        name="gather",
    )(got)
    from_below = from_behind(edge[1], "by", 1)
    from_above = from_behind(edge[0], "by", -1)
    main = main.at[:, :8].add(from_below)
    return main.at[:, 248:].add(from_above)


def solution(mesh):
    return jax.shard_map(
        on_device,
        mesh=mesh,
        in_specs=(P(("bx", "by"), None), P(), P(("bx", "by")), P(("bx", "by")), P(("bx", "by"))),
        out_specs=P("bx", "by", None),
        check_vma=False,
    )
```

time: 1020 us -> 179 us (0.18)
  other arithmetic: 731 us -> 5.93 us
  Pallas kernels: 0 us -> 122 us
  matrix products: 105 us -> 0 us
  local copies, waits for them, and re-layouts: 71.7 us -> 1.28 us
  blocking collectives: 98.9 us -> 38 us
    scatter-add x5 -> x2, other arithmetic: 704 us -> 3.16 us  [the longest x1 1.58 us: on_device(): main = main.at[:, :8].add(from_below)]
    pallas_call x0 -> x2, Pallas kernels: none -> 122 us  [the longest x1 113 us: on_device(): pl.pallas_call(spread_kernel, out_shape=jax.ShapeDtypeStruct((KZ, SENT, 1...]
    dot_general x1 -> x0, matrix products: 63.5 us -> none  [deposit(): jnp.einsum('bkr,brz->bkz', columns, placing, precision=lax.Precision.HIGH...]
    all_to_all x1, blocking collectives: 98.9 us -> 38 us  [on_device(): got = lax.all_to_all(sent, 'bx', split_axis=0, concat_axis=0, tiled=True)]
    dynamic_update_slice x8 -> x0, matrix products: 41.4 us -> none  [one_turn(): return lax.dynamic_update_slice_in_dim(acc, part, begin, 0)]
    slice x8 -> x0, local copies, waits for them, and re-layouts: 27 us -> none  [the longest x2 16.9 us: on_device(): inner = padded[2:CX + 2]]
    select_n x11 -> x0, other arithmetic: 14 us -> none  [the longest x8 12.9 us: one_turn(): jnp.where(pick[:, :, None], qg[:, None, :], jnp.zeros((), qg.dtype))]
    dynamic_slice x16 -> x0, local copies, waits for them, and re-layouts: 12.9 us -> none  [the longest x8 6.81 us: one_turn(): qg = lax.dynamic_slice_in_dim(block_q, begin, group, 0)]
  transfers between devices with their start and end apart: 4 -> 2, of which waited for: 1 -> 2; matrix products, arithmetic and copies ran while one was open for 3% -> 1% of each run, Pallas kernels for 0% -> 0%
where the time goes in v1:
time: 179 us; the launch traced here: 177 us
  Pallas kernels  122 us (68%)
  blocking collectives  38 us (21%)
  other arithmetic  5.93 us (3%)
  starting transfers between devices  5.71 us (3%)
  waiting for transfers between devices  3.97 us (2%)
    pallas_call x1, Pallas kernels, on_device(): pl.pallas_call(spread_kernel, out_shape=jax.ShapeDtypeStruct((KZ, SENT, 1...  113 us
    all_to_all x1, blocking collectives, on_device(): got = lax.all_to_all(sent, 'bx', split_axis=0, concat_axis=0, tiled=True)  38 us
    pallas_call x1, Pallas kernels, on_device(): pl.pallas_call(gather_kernel, out_shape=(jax.ShapeDtypeStruct((8, 256, 51...  8.54 us
    ppermute x2, starting transfers between devices, from_behind(): return lax.ppermute(block, axis, route)  5.71 us
    ppermute x2, waiting for transfers between devices, from_behind(): return lax.ppermute(block, axis, route)  3.97 us
  transfers between devices with their start and end apart: 2, of which 2 were waited for; matrix products, arithmetic and copies ran while one was open for 1% of the time, Pallas kernels for 0%

profile of v1, /device:TPU:0, one launch (start us, length us, event | category | flops | bytes accessed | tf_op | source)
XLA Modules:
  0.0 177.4 jit_solution(7004055508276880696)
XLA Ops:
  0.7 0.7 fusion.9.base_ref
  1.4 0.0 copy-start
  1.4 0.1 reshape.69
  1.5 0.1 copy.12
  1.5 0.8 fusion.2
  2.4 0.5 convert_element_type.6.clash_ref
  2.9 0.7 select_convert_fusion
  3.6 1.1 broadcast_in_dim.4.s_ref
  4.7 0.0 copy-done
  4.7 113.3 %spread.1 = s16[16,624,128]{2,1,0:T(8,128)(2,1)} custom-call(s32[2048]{0:T(1024)} %copy-done, s32[128]{0:T(128)} %convert_element_type.6.clash_ref, s32[1]{0:T(128)} %copy.16.live_ref, bf16[2048,128]{1,0:T(8,128)(2,1)} %q_ref.1, bf16[2048,128]{1,0:T(8,128)(2,1)} %broadcast_in_dim.4.s_ref, bf16[4096,512]{1,0:T(8,128)(2,1)} %bitcast.8, ...), custom_call_target="tpu_custom_call" | custom-call | tf_op jit(solution)/shard_map/spread/pallas_call | solution.py:224
  118.0 38.0 %all_to_all.5.x_ref = s16[16,624,128]{2,1,0:T(8,128)(2,1)S(1)} all-to-all(s16[16,624,128]{2,1,0:T(8,128)(2,1)} %spread.1), channel_id=1, replica_groups=mesh['bx'=16,'by'=8] {'bx'}, dimensions={0} | all-to-all | bytes 5111808 | tf_op jit(solution)/shard_map/all_to_all | solution.py:242
  156.0 8.5 %gather.1 = (f32[8,256,512]{2,1,0:T(8,128)}, f32[2,8,8,512]{3,2,1,0:T(8,128)S(1)}) custom-call(s16[16,624,128]{2,1,0:T(8,128)(2,1)S(1)} %all_to_all.5.x_ref), custom_call_target="tpu_custom_call" | custom-call | tf_op jit(solution)/shard_map/gather/pallas_call | solution.py:243
  164.6 2.7 %collective-permute-start = (f32[8,8,512]{2,1,0:T(8,128)S(1)}, f32[8,8,512]{2,1,0:T(8,128)S(1)}, u32[]{:S(2)}, u32[]{:S(2)}) collective-permute-start(f32[8,8,512]{2,1,0:T(8,128)S(1)} %get-tuple-element.34), channel_id=1, source_target_pairs={{7,0},{0,1},{1,2},{2,3},{3,4},{4,5},{5,6},{6,7},{15,8},{8,9},{9,10... | collective-permute-start | bytes 393224 | tf_op jit(solution)/shard_map/ppermute | solution.py:203
  167.3 3.0 %collective-permute-start.1 = (f32[8,8,512]{2,1,0:T(8,128)S(1)}, f32[8,8,512]{2,1,0:T(8,128)S(1)}, u32[]{:S(2)}, u32[]{:S(2)}) collective-permute-start(f32[8,8,512]{2,1,0:T(8,128)S(1)} %get-tuple-element.33), channel_id=1, source_target_pairs={{1,0},{2,1},{3,2},{4,3},{5,4},{6,5},{7,6},{0,7},{9,8},{10,9},{11,1... | collective-permute-start | bytes 393224 | tf_op jit(solution)/shard_map/ppermute | solution.py:203
  170.3 2.9 %collective-permute-done = f32[8,8,512]{2,1,0:T(8,128)S(1)} collective-permute-done((f32[8,8,512]{2,1,0:T(8,128)S(1)}, f32[8,8,512]{2,1,0:T(8,128)S(1)}, u32[]{:S(2)}, u32[]{:S(2)}) %collective-permute-start) | collective-permute-done | bytes 131104 | tf_op jit(solution)/shard_map/ppermute | solution.py:203
  173.2 1.6 add_dynamic-update-slice_fusion
  174.8 1.0 collective-permute-done.1
  175.8 1.6 fusion
  (1 shorter events, 0.0 us)
Async XLA Ops:
  1.4 3.3 %copy-start = (s32[2048]{0:T(1024)}, s32[2048]{0:T(1024)S(1)}, u32[]{:S(2)}) copy-start(s32[2048]{0:T(1024)S(1)} %fusion.9.base_ref) | copy-start | bytes 24580
  164.6 8.7 %collective-permute-start = (f32[8,8,512]{2,1,0:T(8,128)S(1)}, f32[8,8,512]{2,1,0:T(8,128)S(1)}, u32[]{:S(2)}, u32[]{:S(2)}) collective-permute-start(f32[8,8,512]{2,1,0:T(8,128)S(1)} %get-tuple-element.34), channel_id=1, source_target_pairs={{7,0},{0,1},{1,2},{2,3},{3,4},{4,5},{5,6},{6,7},{15,8},{8,9},{9,10... | collective-permute-start | bytes 393224 | tf_op jit(solution)/shard_map/ppermute | solution.py:203
  167.3 8.5 %collective-permute-start.1 = (f32[8,8,512]{2,1,0:T(8,128)S(1)}, f32[8,8,512]{2,1,0:T(8,128)S(1)}, u32[]{:S(2)}, u32[]{:S(2)}) collective-permute-start(f32[8,8,512]{2,1,0:T(8,128)S(1)} %get-tuple-element.33), channel_id=1, source_target_pairs={{1,0},{2,1},{3,2},{4,3},{5,4},{6,5},{7,6},{0,7},{9,8},{10,9},{11,1... | collective-permute-start | bytes 393224 | tf_op jit(solution)/shard_map/ppermute | solution.py:203

commit v2 on v1

v2 whole, which is shorter than its diff:
```python
import jax
import jax.numpy as jnp
import numpy as np
from jax import lax
from jax.experimental import pallas as pl
from jax.experimental.pallas import tpu as pltpu
from jax.sharding import PartitionSpec as P

NZ = 128
GROUP = 256
BATCH = 16
KZ = 16
UROWS = 24
VSLOTS = 33
FRONT = VSLOTS * UROWS
PLANE = UROWS * VSLOTS
GROWS = FRONT + 4 * KZ * PLANE
SPARE = -GROWS % 256 + 256
VOUT = 34
TAIL = VOUT * 16
SENT = TAIL + 80
WIRE = jnp.int16
LEVELS = 32700.0
UNROLL = 11
SCALE_ROW = TAIL + 34


def restriction():
    coef = [1.0, 4.0, 6.0, 4.0, 1.0]
    table = np.zeros((4, 512, 384), np.float32)
    for p in range(8):
        for mm in range(6):
            tap = p + 4 - 2 * mm
            if not 0 <= tap < 5:
                continue
            for q in range(8):
                for r in range(8):
                    for kind in range(4):
                        z = (r - 2 + 4 * (kind // 2)) % 8
                        y = (q - 2 + 4 * (kind % 2)) % 8
                        table[kind, (p * 8 + q) * 8 + r, mm // 2 * 128 + mm % 2 * 64 + z * 8 + y] = coef[tap] / 8.0
    return np.concatenate([table, table], axis=1).reshape(4096, 384)


def spread_kernel(base_ref, clash_ref, live_ref, q_ref, s_ref, w_ref, r_ref, out_ref, grid_ref, pick_ref, kind_ref, tile_ref, plane_ref):
    k = pl.program_id(0)
    shapes_n = w_ref.shape[0] // 128

    @pl.when(k == 0)
    def _():
        def clear(step, carry):
            grid_ref[pl.ds(pl.multiple_of(step * 256, 256), 256), :] = jnp.zeros((256, 128), jnp.float32)
            return carry

        lax.fori_loop(0, (GROWS + SPARE) // 256, clear, 0)

        def one_group(step, carry):
            begin = pl.multiple_of(step * GROUP, GROUP)
            qg = q_ref[pl.ds(begin, GROUP), :]
            code = s_ref[pl.ds(begin, GROUP), :].astype(jnp.float32)
            whole = jnp.floor(code * 0.25)
            sg = whole.astype(jnp.bfloat16)
            kind = code - 4.0 * whole
            for s in range(shapes_n):
                pick_ref[:, s * 128 : (s + 1) * 128] = jnp.where(sg == s, qg, jnp.zeros_like(qg))
            part = jnp.dot(pick_ref[...], w_ref[...], preferred_element_type=jnp.float32)
            high = part.astype(jnp.bfloat16)
            low = (part - high.astype(jnp.float32)).astype(jnp.bfloat16)
            both = jnp.concatenate([high, low], axis=1)
            kind = jnp.concatenate([kind.astype(jnp.bfloat16)] * 8, axis=1)
            for c in range(4):
                kind_ref[:, c * 1024 : (c + 1) * 1024] = jnp.where(kind == c, both, jnp.zeros_like(both))
            cells = jnp.dot(kind_ref[...], r_ref[...], preferred_element_type=jnp.float32)
            for du in range(3):
                tile_ref[pl.ds(du, GROUP, stride=4), :] = cells[:, du * 128 : (du + 1) * 128]

            def one_batch(batch, inner):
                first = begin + batch * BATCH
                clash = clash_ref[step * (GROUP // BATCH) + batch]
                rows = [base_ref[first + j] for j in range(BATCH)]
                at = [pl.multiple_of(batch * BATCH * 4, 8) + 4 * j for j in range(BATCH)]

                @pl.when(clash == 0)
                def _():
                    sums = [grid_ref[pl.ds(rows[j], 3), :] + tile_ref[pl.ds(at[j], 3), :] for j in range(BATCH)]
                    for j in range(BATCH):
                        grid_ref[pl.ds(rows[j], 3), :] = sums[j]

                @pl.when(clash != 0)
                def _():
                    for j in range(BATCH):
                        grid_ref[pl.ds(rows[j], 3), :] += tile_ref[pl.ds(at[j], 3), :]

                return inner

            return lax.fori_loop(0, GROUP // BATCH, one_batch, carry)

        lax.fori_loop(0, (live_ref[0] + GROUP - 1) // GROUP, one_group, 0)

    lane = lax.broadcasted_iota(jnp.int32, (8, 128), 1)
    z_kept = (lane & 56) < 48
    z_past = (lane & 56) < 16
    y_kept = (lane & 7) < 6
    y_past = (lane & 7) < 2
    next_k = lax.rem(k + 1, KZ)
    last_k = lax.rem(k + KZ - 1, KZ)

    def slab(odd, row, stride=None):
        def at(copy, plane):
            start = pl.multiple_of(FRONT + (copy * KZ + plane) * PLANE, 8) + row
            return grid_ref[pl.ds(start, 8, stride=stride), :]

        return jnp.where(z_kept, at(odd, k), at(odd, next_k)) + jnp.where(z_past, at(2 + odd, last_k), at(2 + odd, k))

    def put(row, value, top):
        plane_ref[pl.ds(row, 8), :] = value
        return jnp.maximum(top, jnp.abs(value))

    def one_slab(v, carry):
        top, evens, odds = carry
        new_evens, new_odds = [], []
        for half in range(2):
            row = pl.multiple_of(v * UROWS, 8) + 8 + 8 * half
            even, odd = slab(0, row), slab(1, row - UROWS)
            value = jnp.where(y_kept, evens[half], even) + jnp.where(y_past, odds[half], odd)
            place = jnp.where(v == 0, VOUT - 2, v - 1)
            top = put(pl.multiple_of(place * 16, 16) + 8 * half, value, top)
            new_evens.append(even)
            new_odds.append(odd)
        return top, tuple(new_evens), tuple(new_odds)

    zero = jnp.zeros((8, 128), jnp.float32)
    top, _, odds = lax.fori_loop(0, VOUT - 1, one_slab, (zero, (zero, zero), (zero, zero)), unroll=UNROLL)
    for half in range(2):
        top = put((VOUT - 1) * 16 + 8 * half, jnp.where(y_past, odds[half], 0.0), top)
    line = lax.broadcasted_iota(jnp.int32, (8, 128), 0)
    for side in range(2):
        for c in range(5):
            row = (8 * c - 1) * UROWS + 7 + side * 17
            even = jnp.where(y_kept, slab(0, row, UROWS), slab(0, row + UROWS, UROWS))
            odd = jnp.where(y_past, slab(1, row - UROWS, UROWS), slab(1, row, UROWS))
            if c == 0:
                odd = jnp.where(line > 0, odd, 0.0)
            if c == 4:
                even = jnp.where(line < 1, even, 0.0)
                odd = jnp.where(line < 2, odd, 0.0)
            top = put(TAIL + side * 40 + c * 8, even + odd, top)
    top = jnp.maximum(jnp.max(top, axis=0, keepdims=True), 1e-37)
    power = jnp.ceil(jnp.log2(top) * 16.0 + 0.01)
    shrink = jnp.exp2(power * -0.0625)
    last = plane_ref[SCALE_ROW - 2 : SCALE_ROW + 6, :]
    whole = jnp.round(plane_ref[...] * shrink * LEVELS)
    out_ref[0] = whole.astype(jnp.int32).astype(out_ref.dtype)
    marked = jnp.where(line == 2, power, jnp.round(last * shrink * LEVELS))
    both = jnp.concatenate([marked, jnp.round(plane_ref[SCALE_ROW + 6 : SCALE_ROW + 14, :] * shrink * LEVELS)], axis=0)
    out_ref[0, SCALE_ROW - 2 : SCALE_ROW + 14, :] = both.astype(jnp.int32).astype(out_ref.dtype)


def take_tails(tails, tail_ref, grow_ref):
    for src in range(16):
        tail = jnp.concatenate([t[src] for t in tails], axis=0).astype(jnp.float32)
        grow = jnp.exp2(tail[SCALE_ROW - TAIL : SCALE_ROW - TAIL + 1] * 0.0625) / LEVELS
        grow_ref[src * 8 : src * 8 + 8, :] = jnp.broadcast_to(grow, (8, 128))
        tail_ref[src * 80 : (src + 1) * 80, :] = tail * grow


def turn(rows_of, slabs, tail_ref, grow_ref, turn_ref):
    lane = lax.broadcasted_iota(jnp.int32, (8, 128), 1)
    line = lax.broadcasted_iota(jnp.int32, (8, 128), 0)
    for src in range(16):
        grow = grow_ref[src * 8 : src * 8 + 8, :]
        halves = []
        for which in range(2):
            both = rows_of(src, which).astype(jnp.float32)
            above = tail_ref[pl.ds((src + 1) % 16 * 80 + slabs[which], 1), :]
            below = tail_ref[pl.ds((src + 15) % 16 * 80 + 40 + slabs[which], 1), :]
            upper = both[0:8] * grow + jnp.where(line == 0, below, 0.0)
            lower = both[8:16] * grow + jnp.where(line == 7, above, 0.0)
            halves.append((upper, lower))
        for half in range(2):
            da, db = halves[0][half], halves[1][half]
            begin = src * 32 + half * 16
            turn_ref[pl.ds(begin, 8, stride=2), :] = jnp.where(lane < 64, da, pltpu.roll(db, 64, 1))
            turn_ref[pl.ds(begin + 1, 8, stride=2), :] = jnp.where(lane < 64, pltpu.roll(da, 64, 1), db)
    return [turn_ref[c * 128 : (c + 1) * 128, :].T.reshape(2, 8, 8, 128) for c in range(4)]


def edge_kernel(low_ref, high_ref, *refs):
    tails, (down_ref, up_ref), scratch = refs[:5], refs[5:7], refs[7:]
    take_tails(tails, *scratch[:2])
    blocks = turn(lambda src, which: (low_ref, high_ref)[which][src], (0, VOUT - 1), *scratch)
    for c, block in enumerate(blocks):
        down_ref[:, :, c * 128 : (c + 1) * 128] = block[0][:, 6:8]
        up_ref[:, :, c * 128 : (c + 1) * 128] = block[1][:, 0:2]


def inner_kernel(x_ref, *refs):
    tails, out_ref, scratch = refs[:5], refs[5], refs[6:]
    step = pl.program_id(0)

    @pl.when(step == 0)
    def _():
        take_tails(tails, *scratch[:2])

    slab = 2 * step + 3
    blocks = turn(lambda src, which: x_ref[src, which * 16 : which * 16 + 16, :], (slab, slab + 1), *scratch)
    for c, block in enumerate(blocks):
        out_ref[:, 0:8, c * 128 : (c + 1) * 128] = block[0]
        out_ref[:, 8:16, c * 128 : (c + 1) * 128] = block[1]


def outer_kernel(x_ref, *refs):
    tails, (below_ref, above_ref, _, out_ref), scratch = refs[:5], refs[5:9], refs[9:]
    step = pl.program_id(0)

    @pl.when(step == 0)
    def _():
        take_tails(tails, *scratch[:2])

    slab = 30 * step + 1
    blocks = turn(lambda src, which: x_ref[src, which * 16 : which * 16 + 16, :], (slab, slab + 1), *scratch)
    for c, block in enumerate(blocks):
        out_ref[:, 0:8, c * 128 : (c + 1) * 128] = block[0]
        out_ref[:, 8:16, c * 128 : (c + 1) * 128] = block[1]

    @pl.when(step == 0)
    def _():
        out_ref[:, 0:2, :] += below_ref[...]

    @pl.when(step == 1)
    def _():
        out_ref[:, 14:16, :] += above_ref[...]


def from_behind(block, axis, distance):
    devices = range(lax.axis_size(axis))
    route = [((i - distance) % len(devices), i) for i in devices]
    return lax.ppermute(block, axis, route)


def on_device(charges, weight_tiles, block_shape, block_box, live_blocks):
    nblk, atoms = charges.shape
    shapes_n, _, cells = weight_tiles.shape
    wflat = weight_tiles.reshape(shapes_n * atoms, cells)
    slot = jnp.arange(nblk, dtype=jnp.int32)
    u = block_box // 2048
    v = block_box // 32 % 64
    w = block_box % 32
    kind = (w % 2) * 2 + v % 2
    base = FRONT + (kind * KZ + w // 2) * PLANE + v // 2 * UROWS + 7 + u
    code = jnp.where(slot < live_blocks[0], block_shape, shapes_n) * 4 + kind
    code = jnp.broadcast_to(code.astype(jnp.bfloat16)[:, None], (nblk, 128))
    batched = base.reshape(nblk // BATCH, BATCH).T
    near = jnp.abs(batched[:, None, :] - batched[None, :, :]) < 3
    order = np.arange(BATCH)[:, None] < np.arange(BATCH)[None, :]
    clash = jnp.any(near & order[:, :, None], axis=(0, 1)).astype(jnp.int32)

    whole = lambda shp: pl.BlockSpec(shp, lambda k, *_: (0,) * len(shp), pipeline_mode=pl.Buffered(1))
    sent = pl.pallas_call(
        spread_kernel,
        out_shape=jax.ShapeDtypeStruct((KZ, SENT, 128), WIRE),
        grid_spec=pltpu.PrefetchScalarGridSpec(
            num_scalar_prefetch=3,
            grid=(KZ,),
            in_specs=[whole((nblk, 128)), whole((nblk, 128)), whole((shapes_n * atoms, cells)), whole((4096, 384))],
            out_specs=pl.BlockSpec((1, SENT, 128), lambda k, *_: (k, 0, 0)),
            scratch_shapes=[
                pltpu.VMEM((GROWS + SPARE, 128), jnp.float32),
                pltpu.VMEM((GROUP, shapes_n * atoms), jnp.bfloat16),
                pltpu.VMEM((GROUP, 4096), jnp.bfloat16),
                pltpu.VMEM((GROUP * 4, 128), jnp.float32),
                pltpu.VMEM((SENT, 128), jnp.float32),
            ],
        ),
        compiler_params=pltpu.CompilerParams(vmem_limit_bytes=56 * 1024 * 1024),
        name="spread",
    )(base, clash, live_blocks, charges, code, wflat, jnp.asarray(restriction(), jnp.bfloat16))
    got = lax.all_to_all(sent, "bx", split_axis=0, concat_axis=0, tiled=True)
    piece = lambda i: pl.BlockSpec((KZ, 16, 128), lambda p: (0, i, 0))
    tails = [piece(TAIL // 16 + i) for i in range(5)]
    small = pl.BlockSpec((8, 2, 512), lambda p: (0, 0, 0))
    full = jax.ShapeDtypeStruct((8, 256, 512), jnp.float32)
    scratch = [
        pltpu.VMEM((16 * 80, 128), jnp.float32),
        pltpu.VMEM((128, 128), jnp.float32),
        pltpu.VMEM((512, 128), jnp.float32),
    ]
    params = pltpu.CompilerParams(vmem_limit_bytes=40 * 1024 * 1024)
    down, up = pl.pallas_call(
        edge_kernel,
        out_shape=(jax.ShapeDtypeStruct((8, 2, 512), jnp.float32),) * 2,
        grid=(1,),
        in_specs=[piece(VOUT - 2), piece(VOUT - 1)] + tails,
        out_specs=(small, small),
        scratch_shapes=scratch,
        compiler_params=params,
        name="edge",
    )(*[got] * 7)
    below = from_behind(up, "by", 1)
    above = from_behind(down, "by", -1)
    inner = pl.pallas_call(
        inner_kernel,
        out_shape=full,
        grid=(14,),
        in_specs=[pl.BlockSpec((KZ, 32, 128), lambda p: (0, p + 1, 0))] + tails,
        out_specs=pl.BlockSpec((8, 16, 512), lambda p: (0, p + 1, 0)),
        scratch_shapes=scratch,
        compiler_params=params,
        name="inner",
    )(*[got] * 6)
    return pl.pallas_call(
        outer_kernel,
        out_shape=full,
        grid=(2,),
        in_specs=[pl.BlockSpec((KZ, 32, 128), lambda p: (0, 15 * p, 0))]
        + tails
        + [small, small, pl.BlockSpec(memory_space=pl.ANY)],
        out_specs=pl.BlockSpec((8, 16, 512), lambda p: (0, 15 * p, 0)),
        scratch_shapes=scratch,
        input_output_aliases={8: 0},
        compiler_params=params,
        name="outer",
    )(*[got] * 6, below, above, inner)


def solution(mesh):
    return jax.shard_map(
        on_device,
        mesh=mesh,
        in_specs=(P(("bx", "by"), None), P(), P(("bx", "by")), P(("bx", "by")), P(("bx", "by"))),
        out_specs=P("bx", "by", None),
        check_vma=False,
    )
```

time: 179 us -> 98.2 us (0.55)
  Pallas kernels: 122 us -> 27.6 us
  blocking collectives: 38 us -> 60.9 us
  waiting for transfers between devices: 3.97 us -> 0.01 us
  other arithmetic: 5.93 us -> 2.16 us
    pallas_call x1, Pallas kernels: 113 us -> 18.4 us  [on_device(): pl.pallas_call(spread_kernel, out_shape=jax.ShapeDtypeStruct((KZ, SENT, 1...]
    all_to_all x1, blocking collectives: 38 us -> 60.9 us  [on_device(): got = lax.all_to_all(sent, 'bx', split_axis=0, concat_axis=0, tiled=True)]
    ppermute x2, waiting for transfers between devices: 3.97 us -> 0.01 us  [from_behind(): return lax.ppermute(block, axis, route)]
    scatter-add x2 -> x0, other arithmetic: 3.16 us -> none  [the longest x1 1.58 us: on_device(): main = main.at[:, :8].add(from_below)]
    pallas_call x1 -> x3, Pallas kernels: 8.54 us -> 9.15 us  [the longest x1 7.34 us: on_device(): pl.pallas_call(inner_kernel, out_shape=full, grid=(14,), in_specs=[pl.Blo...]
  transfers between devices with their start and end apart: 2 -> 2, of which waited for: 2 -> 0; matrix products, arithmetic and copies ran while one was open for 1% -> 0% of each run, Pallas kernels for 0% -> 7%
where the time goes in v2:
time: 98.2 us; the launch traced here: 98.3 us
  blocking collectives  60.9 us (62%)
  Pallas kernels  27.6 us (28%)
  starting transfers between devices  5.71 us (6%)
  other arithmetic  2.16 us (2%)
  local copies, waits for them, and re-layouts  1.26 us (1%)
    all_to_all x1, blocking collectives, on_device(): got = lax.all_to_all(sent, 'bx', split_axis=0, concat_axis=0, tiled=True)  60.9 us
    pallas_call x1, Pallas kernels, on_device(): pl.pallas_call(spread_kernel, out_shape=jax.ShapeDtypeStruct((KZ, SENT, 1...  18.4 us
    pallas_call x1, Pallas kernels, on_device(): pl.pallas_call(inner_kernel, out_shape=full, grid=(14,), in_specs=[pl.Blo...  7.34 us
    ppermute x2, starting transfers between devices, from_behind(): return lax.ppermute(block, axis, route)  5.71 us
  transfers between devices with their start and end apart: 2, of which 0 were waited for; matrix products, arithmetic and copies ran while one was open for 0% of the time, Pallas kernels for 7%

profile of v2, /device:TPU:0, one launch (start us, length us, event | category | flops | bytes accessed | tf_op | source)
XLA Modules:
  0.0 98.3 jit_solution(861573388683093692)
XLA Ops:
  0.7 0.8 add_convert_fusion
  1.4 0.0 copy-start
  1.4 0.1 reshape.9
  1.5 0.1 copy.13
  1.6 0.8 fusion.1
  2.4 0.6 convert_element_type.6.clash_ref
  3.0 1.1 %broadcast_in_dim.4.s_ref = bf16[2048,128]{1,0:T(8,128)(2,1)} broadcast(bf16[2048]{0:T(1024)(128)(2,1)S(1)} %get-tuple-element.9), dimensions={0} | broadcast | bytes 528384 | tf_op jit(solution)/shard_map/broadcast_in_dim | solution.py:252
  4.1 0.0 copy-done
  4.1 18.4 %spread.1 = s16[16,624,128]{2,1,0:T(8,128)(2,1)} custom-call(s32[2048]{0:T(1024)} %copy-done, s32[128]{0:T(128)} %convert_element_type.6.clash_ref, s32[1]{0:T(128)} %copy.16.live_ref, bf16[2048,128]{1,0:T(8,128)(2,1)} %q_ref.1, bf16[2048,128]{1,0:T(8,128)(2,1)} %broadcast_in_dim.4.s_ref, bf16[4096,512]{1,0:T(8,128)(2,1)} %bitcast.4, ...), custom_call_target="tpu_custom_call" | custom-call | tf_op jit(solution)/shard_map/spread/pallas_call | solution.py:259
  22.5 60.9 %all_to_all.5.low_ref.high_ref.refs_0_.refs_1_.refs_2_.refs_3_.refs_4_.x_ref = s16[16,624,128]{2,1,0:T(8,128)(2,1)S(1)} all-to-all(s16[16,624,128]{2,1,0:T(8,128)(2,1)} %spread.1), channel_id=1, replica_groups=mesh['bx'=16,'by'=8] {'bx'}, dimensions={0} | all-to-all | bytes 5111808 | tf_op jit(solution)/shard_map/all_to_all | solution.py:278
  83.4 0.3 edge.1
  83.7 0.3 collective-permute-start
  84.0 5.4 %collective-permute-start.1 = (f32[8,2,512]{2,1,0:T(2,128)S(1)}, f32[8,2,512]{2,1,0:T(2,128)S(1)}, u32[]{:S(2)}, u32[]{:S(2)}) collective-permute-start(f32[8,2,512]{2,1,0:T(2,128)S(1)} %get-tuple-element.8), channel_id=1, source_target_pairs={{1,0},{2,1},{3,2},{4,3},{5,4},{6,5},{7,6},{0,7},{9,8},{10,9},{11,1... | collective-permute-start | bytes 98312 | tf_op jit(solution)/shard_map/ppermute | solution.py:238
  89.4 7.3 %inner.1.refs_7_ = f32[8,256,512]{2,1,0:T(8,128)} custom-call(s16[16,624,128]{2,1,0:T(8,128)(2,1)S(1)} %all_to_all.5.low_ref.high_ref.refs_0_.refs_1_.refs_2_.refs_3_.refs_4_.x_ref, s16[16,624,128]{2,1,0:T(8,128)(2,1)S(1)} %all_to_all.5.low_ref.high_ref.refs_0_.refs_1_.refs_2_.refs_3_.refs_4_.x_ref, ...), custom_call_target="tpu_custom_call" | custom-call | tf_op jit(solution)/shard_map/inner/pallas_call | solution.py:301
  96.8 0.0 collective-permute-done.refs_5_
  96.8 0.0 collective-permute-done.1.refs_6_
  96.8 1.5 %outer.1 = f32[8,256,512]{2,1,0:T(8,128)} custom-call(s16[16,624,128]{2,1,0:T(8,128)(2,1)S(1)} %all_to_all.5.low_ref.high_ref.refs_0_.refs_1_.refs_2_.refs_3_.refs_4_.x_ref, s16[16,624,128]{2,1,0:T(8,128)(2,1)S(1)} %all_to_all.5.low_ref.high_ref.refs_0_.refs_1_.refs_2_.refs_3_.refs_4_.x_ref, ...), custom_call_target="tpu_custom_call", output_to_operand_aliasing={{}: (8, {})} | custom-call | tf_op jit(solution)/shard_map/outer/pallas_call | solution.py:311
Async XLA Ops:
  1.4 2.7 %copy-start = (s32[2048]{0:T(1024)}, s32[2048]{0:T(1024)S(1)}, u32[]{:S(2)}) copy-start(s32[2048]{0:T(1024)S(1)} %get-tuple-element.10.base_ref) | copy-start | bytes 24580
  83.7 13.1 %collective-permute-start = (f32[8,2,512]{2,1,0:T(2,128)S(1)}, f32[8,2,512]{2,1,0:T(2,128)S(1)}, u32[]{:S(2)}, u32[]{:S(2)}) collective-permute-start(f32[8,2,512]{2,1,0:T(2,128)S(1)} %get-tuple-element.7), channel_id=1, source_target_pairs={{7,0},{0,1},{1,2},{2,3},{3,4},{4,5},{5,6},{6,7},{15,8},{8,9},{9,10... | collective-permute-start | bytes 98312 | tf_op jit(solution)/shard_map/ppermute | solution.py:238
  84.0 12.8 %collective-permute-start.1 = (f32[8,2,512]{2,1,0:T(2,128)S(1)}, f32[8,2,512]{2,1,0:T(2,128)S(1)}, u32[]{:S(2)}, u32[]{:S(2)}) collective-permute-start(f32[8,2,512]{2,1,0:T(2,128)S(1)} %get-tuple-element.8), channel_id=1, source_target_pairs={{1,0},{2,1},{3,2},{4,3},{5,4},{6,5},{7,6},{0,7},{9,8},{10,9},{11,1... | collective-permute-start | bytes 98312 | tf_op jit(solution)/shard_map/ppermute | solution.py:238

commit v3 on v2

--- a/solution.py
+++ b/solution.py
@@ -16,6 +16,7 @@
 PLANE = UROWS * VSLOTS
 GROWS = FRONT + 4 * KZ * PLANE
 SPARE = -GROWS % 256 + 256
+DUMP = GROWS + SPARE - 8
 VOUT = 34
 TAIL = VOUT * 16
 SENT = TAIL + 80
@@ -27,7 +28,7 @@
 
 def restriction():
     coef = [1.0, 4.0, 6.0, 4.0, 1.0]
-    table = np.zeros((4, 512, 384), np.float32)
+    table = np.zeros((2, 512, 384), np.float32)
     for p in range(8):
         for mm in range(6):
             tap = p + 4 - 2 * mm
@@ -35,71 +36,121 @@
                 continue
             for q in range(8):
                 for r in range(8):
-                    for kind in range(4):
-                        z = (r - 2 + 4 * (kind // 2)) % 8
-                        y = (q - 2 + 4 * (kind % 2)) % 8
-                        table[kind, (p * 8 + q) * 8 + r, mm // 2 * 128 + mm % 2 * 64 + z * 8 + y] = coef[tap] / 8.0
-    return np.concatenate([table, table], axis=1).reshape(4096, 384)
-
-
-def spread_kernel(base_ref, clash_ref, live_ref, q_ref, s_ref, w_ref, r_ref, out_ref, grid_ref, pick_ref, kind_ref, tile_ref, plane_ref):
-    k = pl.program_id(0)
+                    z = (r - 2) % 8
+                    for odd in range(2):
+                        y = (q - 2 + 4 * odd) % 8
+                        lane = z // 4 * 64 + mm % 2 * 32 + z % 4 * 8 + y
+                        table[odd, (p * 8 + q) * 8 + r, mm // 2 * 128 + lane] = coef[tap] / 8.0
+    return np.concatenate([table, table], axis=1).reshape(2048, 384)
+
+
+def spread_kernel(base_ref, fast_ref, clash_ref, live_ref, q_ref, code_ref, w_any, r_any, out_ref, *scratch):
+    grid_ref, w_ref, r_ref, pick_ref, kind_ref, tile_a, tile_b, plane_ref, sems = scratch
     shapes_n = w_ref.shape[0] // 128
-
-    @pl.when(k == 0)
-    def _():
-        def clear(step, carry):
-            grid_ref[pl.ds(pl.multiple_of(step * 256, 256), 256), :] = jnp.zeros((256, 128), jnp.float32)
-            return carry
-
-        lax.fori_loop(0, (GROWS + SPARE) // 256, clear, 0)
-
-        def one_group(step, carry):
-            begin = pl.multiple_of(step * GROUP, GROUP)
-            qg = q_ref[pl.ds(begin, GROUP), :]
-            code = s_ref[pl.ds(begin, GROUP), :].astype(jnp.float32)
-            whole = jnp.floor(code * 0.25)
-            sg = whole.astype(jnp.bfloat16)
-            kind = code - 4.0 * whole
-            for s in range(shapes_n):
-                pick_ref[:, s * 128 : (s + 1) * 128] = jnp.where(sg == s, qg, jnp.zeros_like(qg))
-            part = jnp.dot(pick_ref[...], w_ref[...], preferred_element_type=jnp.float32)
-            high = part.astype(jnp.bfloat16)
-            low = (part - high.astype(jnp.float32)).astype(jnp.bfloat16)
-            both = jnp.concatenate([high, low], axis=1)
-            kind = jnp.concatenate([kind.astype(jnp.bfloat16)] * 8, axis=1)
-            for c in range(4):
-                kind_ref[:, c * 1024 : (c + 1) * 1024] = jnp.where(kind == c, both, jnp.zeros_like(both))
-            cells = jnp.dot(kind_ref[...], r_ref[...], preferred_element_type=jnp.float32)
-            for du in range(3):
-                tile_ref[pl.ds(du, GROUP, stride=4), :] = cells[:, du * 128 : (du + 1) * 128]
-
-            def one_batch(batch, inner):
-                first = begin + batch * BATCH
-                clash = clash_ref[step * (GROUP // BATCH) + batch]
-                rows = [base_ref[first + j] for j in range(BATCH)]
-                at = [pl.multiple_of(batch * BATCH * 4, 8) + 4 * j for j in range(BATCH)]
-
-                @pl.when(clash == 0)
+    w_copy = pltpu.make_async_copy(w_any, w_ref, sems.at[0])
+    r_copy = pltpu.make_async_copy(r_any, r_ref, sems.at[1])
+    w_copy.start()
+    r_copy.start()
+    tile_b[...] = jnp.zeros(tile_b.shape, jnp.float32)
+
+    def clear(step, carry):
+        grid_ref[pl.ds(pl.multiple_of(step * 256, 256), 256), :] = jnp.zeros((256, 128), jnp.float32)
+        return carry
+
+    lax.fori_loop(0, (GROWS + SPARE) // 256, clear, 0)
+    w_copy.wait()
+    r_copy.wait()
+
+    def product(step, tile_ref):
+        begin = pl.multiple_of(step * GROUP, GROUP)
+        qg = q_ref[pl.ds(begin, GROUP), :]
+        codes = [code_ref[pl.ds(step * (GROUP // 128) + h, 1), :] for h in range(GROUP // 128)]
+        code = jnp.concatenate([jnp.broadcast_to(c, (128, 128)).T for c in codes], axis=0)
+        whole = jnp.floor(code * 0.25)
+        sg = whole.astype(jnp.bfloat16)
+        kind = code - 4.0 * whole
+        z_odd = kind >= 2.0
+        y_odd = jnp.where(z_odd, kind - 2.0, kind).astype(jnp.bfloat16)
+        for s in range(shapes_n):
+            pick_ref[:, s * 128 : (s + 1) * 128] = jnp.where(sg == s, qg, jnp.zeros_like(qg))
+        part = jnp.dot(pick_ref[...], w_ref[...], preferred_element_type=jnp.float32)
+        high = part.astype(jnp.bfloat16)
+        low = (part - high.astype(jnp.float32)).astype(jnp.bfloat16)
+        both = jnp.concatenate([high, low], axis=1)
+        y_odd = jnp.concatenate([y_odd] * 8, axis=1)
+        for c in range(2):
+            kind_ref[:, c * 1024 : (c + 1) * 1024] = jnp.where(y_odd == c, both, jnp.zeros_like(both))
+        cells = jnp.dot(kind_ref[...], r_ref[...], preferred_element_type=jnp.float32)
+        for du in range(3):
+            rows = cells[:, du * 128 : (du + 1) * 128]
+            tile_ref[pl.ds(du, GROUP, stride=4), :] = jnp.where(z_odd, pltpu.roll(rows, 64, 1), rows)
+
+    def deposit(step, tile_ref):
+        for batch in range(GROUP // BATCH):
+            first = step * GROUP + batch * BATCH
+            rows = [fast_ref[first + j] for j in range(BATCH)]
+            at = [(batch * BATCH + j) * 4 for j in range(BATCH)]
+            sums = [grid_ref[pl.ds(rows[j], 3), :] + tile_ref[at[j] : at[j] + 3, :] for j in range(BATCH)]
+            for j in range(BATCH):
+                grid_ref[pl.ds(rows[j], 3), :] = sums[j]
+
+    def deposit_rest(step, tile_ref):
+        flag = clash_ref[step * (GROUP // BATCH)]
+        for batch in range(1, GROUP // BATCH):
+            flag = flag | clash_ref[step * (GROUP // BATCH) + batch]
+
+        @pl.when(flag != 0)
+        def _():
+            def one_batch(batch, carry):
+                @pl.when(clash_ref[step * (GROUP // BATCH) + batch] != 0)
                 def _():
-                    sums = [grid_ref[pl.ds(rows[j], 3), :] + tile_ref[pl.ds(at[j], 3), :] for j in range(BATCH)]
-                    for j in range(BATCH):
-                        grid_ref[pl.ds(rows[j], 3), :] = sums[j]
-
-                @pl.when(clash != 0)
-                def _():
-                    for j in range(BATCH):
-                        grid_ref[pl.ds(rows[j], 3), :] += tile_ref[pl.ds(at[j], 3), :]
-
-                return inner
-
-            return lax.fori_loop(0, GROUP // BATCH, one_batch, carry)
-
-        lax.fori_loop(0, (live_ref[0] + GROUP - 1) // GROUP, one_group, 0)
-
+                    def one_block(j, inner):
+                        slot = step * GROUP + batch * BATCH + j
+
+                        @pl.when(fast_ref[slot] != base_ref[slot])
+                        def _():
+                            tile = tile_ref[pl.ds((batch * BATCH + j) * 4, 3), :]
+                            grid_ref[pl.ds(base_ref[slot], 3), :] += tile
+
+                        return inner
+
+                    lax.fori_loop(0, BATCH, one_block, 0)
+
+                return carry
+
+            lax.fori_loop(0, GROUP // BATCH, one_batch, 0)
+
+    def two_groups(pair, carry):
+        before = jnp.maximum(2 * pair - 1, 0)
+        product(2 * pair, tile_a)
+        deposit(before, tile_b)
+
+        @pl.when(pair > 0)
+        def _():
+            deposit_rest(before, tile_b)
+
+        product(2 * pair + 1, tile_b)
+        deposit(2 * pair, tile_a)
+        deposit_rest(2 * pair, tile_a)
+        return carry
+
+    pairs = (live_ref[0] + 2 * GROUP - 1) // (2 * GROUP)
+    lax.fori_loop(0, pairs, two_groups, 0)
+    deposit(2 * pairs - 1, tile_b)
+    deposit_rest(2 * pairs - 1, tile_b)
+
+    def one_plane(k, carry):
+        combine(k, grid_ref, plane_ref, out_ref)
+        return carry
+
+    lax.fori_loop(0, KZ, one_plane, 0)
+
+
+def combine(k, grid_ref, plane_ref, out_ref):
     lane = lax.broadcasted_iota(jnp.int32, (8, 128), 1)
-    z_kept = (lane & 56) < 48
-    z_past = (lane & 56) < 16
+    z = ((lane >> 6) << 2) + ((lane >> 3) & 3)
+    z_kept = z < 6
+    z_past = z < 2
     y_kept = (lane & 7) < 6
     y_past = (lane & 7) < 2
     next_k = lax.rem(k + 1, KZ)
@@ -150,10 +201,10 @@
     shrink = jnp.exp2(power * -0.0625)
     last = plane_ref[SCALE_ROW - 2 : SCALE_ROW + 6, :]
     whole = jnp.round(plane_ref[...] * shrink * LEVELS)
-    out_ref[0] = whole.astype(jnp.int32).astype(out_ref.dtype)
+    out_ref[k] = whole.astype(jnp.int32).astype(out_ref.dtype)
     marked = jnp.where(line == 2, power, jnp.round(last * shrink * LEVELS))
     both = jnp.concatenate([marked, jnp.round(plane_ref[SCALE_ROW + 6 : SCALE_ROW + 14, :] * shrink * LEVELS)], axis=0)
-    out_ref[0, SCALE_ROW - 2 : SCALE_ROW + 14, :] = both.astype(jnp.int32).astype(out_ref.dtype)
+    out_ref[k, SCALE_ROW - 2 : SCALE_ROW + 14, :] = both.astype(jnp.int32).astype(out_ref.dtype)
 
 
 def take_tails(tails, tail_ref, grow_ref):
@@ -180,9 +231,13 @@
         for half in range(2):
             da, db = halves[0][half], halves[1][half]
             begin = src * 32 + half * 16
-            turn_ref[pl.ds(begin, 8, stride=2), :] = jnp.where(lane < 64, da, pltpu.roll(db, 64, 1))
-            turn_ref[pl.ds(begin + 1, 8, stride=2), :] = jnp.where(lane < 64, pltpu.roll(da, 64, 1), db)
-    return [turn_ref[c * 128 : (c + 1) * 128, :].T.reshape(2, 8, 8, 128) for c in range(4)]
+            turn_ref[pl.ds(begin, 8, stride=2), :] = jnp.where(lane & 32 == 0, da, pltpu.roll(db, 32, 1))
+            turn_ref[pl.ds(begin + 1, 8, stride=2), :] = jnp.where(lane & 32 == 0, pltpu.roll(da, 96, 1), db)
+    blocks = []
+    for c in range(4):
+        block = turn_ref[c * 128 : (c + 1) * 128, :].T.reshape(2, 2, 4, 8, 128)
+        blocks.append([jnp.concatenate([block[0, which], block[1, which]], axis=0) for which in range(2)])
+    return blocks
 
 
 def edge_kernel(low_ref, high_ref, *refs):
@@ -249,32 +304,36 @@
     kind = (w % 2) * 2 + v % 2
     base = FRONT + (kind * KZ + w // 2) * PLANE + v // 2 * UROWS + 7 + u
     code = jnp.where(slot < live_blocks[0], block_shape, shapes_n) * 4 + kind
-    code = jnp.broadcast_to(code.astype(jnp.bfloat16)[:, None], (nblk, 128))
+    code = code.astype(jnp.float32).reshape(nblk // 128, 128)
     batched = base.reshape(nblk // BATCH, BATCH).T
     near = jnp.abs(batched[:, None, :] - batched[None, :, :]) < 3
-    order = np.arange(BATCH)[:, None] < np.arange(BATCH)[None, :]
-    clash = jnp.any(near & order[:, :, None], axis=(0, 1)).astype(jnp.int32)
-
-    whole = lambda shp: pl.BlockSpec(shp, lambda k, *_: (0,) * len(shp), pipeline_mode=pl.Buffered(1))
+    earlier = np.arange(BATCH)[:, None] < np.arange(BATCH)[None, :]
+    late = jnp.any(near & earlier[:, :, None], axis=0)
+    fast = jnp.where(late, DUMP, batched).T.reshape(nblk)
+    clash = jnp.any(late, axis=0).astype(jnp.int32)
+
+    vmem = pl.BlockSpec(memory_space=pltpu.VMEM)
+    smem = pl.BlockSpec(memory_space=pltpu.SMEM)
+    hbm = pl.BlockSpec(memory_space=pl.ANY)
     sent = pl.pallas_call(
         spread_kernel,
         out_shape=jax.ShapeDtypeStruct((KZ, SENT, 128), WIRE),
-        grid_spec=pltpu.PrefetchScalarGridSpec(
-            num_scalar_prefetch=3,
-            grid=(KZ,),
-            in_specs=[whole((nblk, 128)), whole((nblk, 128)), whole((shapes_n * atoms, cells)), whole((4096, 384))],
-            out_specs=pl.BlockSpec((1, SENT, 128), lambda k, *_: (k, 0, 0)),
-            scratch_shapes=[
-                pltpu.VMEM((GROWS + SPARE, 128), jnp.float32),
-                pltpu.VMEM((GROUP, shapes_n * atoms), jnp.bfloat16),
-                pltpu.VMEM((GROUP, 4096), jnp.bfloat16),
-                pltpu.VMEM((GROUP * 4, 128), jnp.float32),
-                pltpu.VMEM((SENT, 128), jnp.float32),
-            ],
-        ),
+        in_specs=[smem] * 4 + [vmem] * 2 + [hbm] * 2,
+        out_specs=vmem,
+        scratch_shapes=[
+            pltpu.VMEM((GROWS + SPARE, 128), jnp.float32),
+            pltpu.VMEM((shapes_n * atoms, cells), jnp.bfloat16),
+            pltpu.VMEM((2048, 384), jnp.bfloat16),
+            pltpu.VMEM((GROUP, shapes_n * atoms), jnp.bfloat16),
+            pltpu.VMEM((GROUP, 2048), jnp.bfloat16),
+            pltpu.VMEM((GROUP * 4, 128), jnp.float32),
+            pltpu.VMEM((GROUP * 4, 128), jnp.float32),
+            pltpu.VMEM((SENT, 128), jnp.float32),
+            pltpu.SemaphoreType.DMA((2,)),
+        ],
         compiler_params=pltpu.CompilerParams(vmem_limit_bytes=56 * 1024 * 1024),
         name="spread",
-    )(base, clash, live_blocks, charges, code, wflat, jnp.asarray(restriction(), jnp.bfloat16))
+    )(base, fast, clash, live_blocks, charges, code, wflat, jnp.asarray(restriction(), jnp.bfloat16))
     got = lax.all_to_all(sent, "bx", split_axis=0, concat_axis=0, tiled=True)
     piece = lambda i: pl.BlockSpec((KZ, 16, 128), lambda p: (0, i, 0))
     tails = [piece(TAIL // 16 + i) for i in range(5)]

time: 98.2 us -> 90.7 us (0.924)
  blocking collectives: 60.9 us -> 41.5 us
  Pallas kernels: 27.6 us -> 39.5 us
    all_to_all x1, blocking collectives: 60.9 us -> 41.5 us  [on_device(): got = lax.all_to_all(sent, 'bx', split_axis=0, concat_axis=0, tiled=True)]
    pallas_call x1, Pallas kernels: 18.4 us -> 30.3 us  [on_device(): pl.pallas_call(spread_kernel, out_shape=jax.ShapeDtypeStruct((KZ, SENT, 1...]
    reshape x0 -> x1, other arithmetic: none -> 1.34 us  [on_device(): code = code.astype(jnp.float32).reshape(nblk // 128, 128)]
    broadcast_in_dim x1 -> x0, local copies, waits for them, and re-layouts: 1.13 us -> none  [on_device(): code = jnp.broadcast_to(code.astype(jnp.bfloat16)[:, None], (nblk, 128))]
  transfers between devices with their start and end apart: 2 -> 2, of which waited for: 0 -> 0; matrix products, arithmetic and copies ran while one was open for 0% -> 0% of each run, Pallas kernels for 7% -> 8%
where the time goes in v3:
time: 90.7 us; the launch traced here: 91 us
  blocking collectives  41.5 us (46%)
  Pallas kernels  39.5 us (44%)
  starting transfers between devices  5.71 us (6%)
  other arithmetic  2.69 us (3%)
  local copies, waits for them, and re-layouts  0.98 us (1%)
    all_to_all x1, blocking collectives, on_device(): got = lax.all_to_all(sent, 'bx', split_axis=0, concat_axis=0, tiled=True)  41.5 us
    pallas_call x1, Pallas kernels, on_device(): pl.pallas_call(spread_kernel, out_shape=jax.ShapeDtypeStruct((KZ, SENT, 1...  30.3 us
    pallas_call x1, Pallas kernels, on_device(): pl.pallas_call(inner_kernel, out_shape=full, grid=(14,), in_specs=[pl.Blo...  7.33 us
    ppermute x2, starting transfers between devices, from_behind(): return lax.ppermute(block, axis, route)  5.71 us
  transfers between devices with their start and end apart: 2, of which 0 were waited for; matrix products, arithmetic and copies ran while one was open for 0% of the time, Pallas kernels for 8%

profile of v3, /device:TPU:0, one launch (start us, length us, event | category | flops | bytes accessed | tf_op | source)
XLA Modules:
  0.0 91.0 jit_solution(14623244473103518145)
XLA Ops:
  0.7 1.3 %convert_bitcast_fusion = (f32[16,128]{1,0:T(8,128)}, s32[2048]{0:T(1024)S(1)}) fusion(s32[2048]{0:T(1024)} %param.9, s32[]{:T(128)} %bitcast.7, s32[2048]{0:T(1024)} %param.10), kind=kLoop, calls=%fused_computation.36 | loop fusion | flops 190464 | bytes 32772 | tf_op jit(solution)/shard_map/reshape | solution.py:307
  2.0 0.0 copy-start
  2.0 0.1 reshape.14
  2.1 0.1 copy.15
  2.1 0.1 copy.13
  2.2 0.8 fusion.1
  3.0 0.5 convert_element_type.6.clash_ref
  3.6 0.1 copy.16
  3.7 0.7 reshape.15.fast_ref
  4.3 0.0 copy-done
  4.3 30.3 %spread.1 = s16[16,624,128]{2,1,0:T(8,128)(2,1)} custom-call(s32[2048]{0:T(1024)} %copy-done, s32[2048]{0:T(1024)} %reshape.15.fast_ref, s32[128]{0:T(128)} %convert_element_type.6.clash_ref, s32[1]{0:T(128)} %copy.18.live_ref, bf16[2048,128]{1,0:T(8,128)(2,1)} %q_ref.1, f32[16,128]{1,0:T(8,128)} %get-tuple-element.11.code_ref, bf16[4096,512]{1,0:T(8,128)(2,1)} %bitcast.8, ...), custom_call_target="tpu_custom_call" | custom-call | tf_op jit(solution)/shard_map/spread/pallas_call | solution.py:318
  34.7 41.5 %all_to_all.5.low_ref.high_ref.refs_0_.refs_1_.refs_2_.refs_3_.refs_4_.x_ref = s16[16,624,128]{2,1,0:T(8,128)(2,1)S(1)} all-to-all(s16[16,624,128]{2,1,0:T(8,128)(2,1)} %spread.1), channel_id=1, replica_groups=mesh['bx'=16,'by'=8] {'bx'}, dimensions={0} | all-to-all | bytes 5111808 | tf_op jit(solution)/shard_map/all_to_all | solution.py:337
  76.1 0.3 edge.1
  76.5 1.8 %collective-permute-start = (f32[8,2,512]{2,1,0:T(2,128)S(1)}, f32[8,2,512]{2,1,0:T(2,128)S(1)}, u32[]{:S(2)}, u32[]{:S(2)}) collective-permute-start(f32[8,2,512]{2,1,0:T(2,128)S(1)} %get-tuple-element.7), channel_id=1, source_target_pairs={{7,0},{0,1},{1,2},{2,3},{3,4},{4,5},{5,6},{6,7},{15,8},{8,9},{9,10... | collective-permute-start | bytes 98312 | tf_op jit(solution)/shard_map/ppermute | solution.py:293
  78.3 3.9 %collective-permute-start.1 = (f32[8,2,512]{2,1,0:T(2,128)S(1)}, f32[8,2,512]{2,1,0:T(2,128)S(1)}, u32[]{:S(2)}, u32[]{:S(2)}) collective-permute-start(f32[8,2,512]{2,1,0:T(2,128)S(1)} %get-tuple-element.8), channel_id=1, source_target_pairs={{1,0},{2,1},{3,2},{4,3},{5,4},{6,5},{7,6},{0,7},{9,8},{10,9},{11,1... | collective-permute-start | bytes 98312 | tf_op jit(solution)/shard_map/ppermute | solution.py:293
  82.2 7.3 %inner.1.refs_7_ = f32[8,256,512]{2,1,0:T(8,128)} custom-call(s16[16,624,128]{2,1,0:T(8,128)(2,1)S(1)} %all_to_all.5.low_ref.high_ref.refs_0_.refs_1_.refs_2_.refs_3_.refs_4_.x_ref, s16[16,624,128]{2,1,0:T(8,128)(2,1)S(1)} %all_to_all.5.low_ref.high_ref.refs_0_.refs_1_.refs_2_.refs_3_.refs_4_.x_ref, ...), custom_call_target="tpu_custom_call" | custom-call | tf_op jit(solution)/shard_map/inner/pallas_call | solution.py:360
  89.5 0.0 collective-permute-done.refs_5_
  89.5 0.0 collective-permute-done.1.refs_6_
  89.5 1.5 %outer.1 = f32[8,256,512]{2,1,0:T(8,128)} custom-call(s16[16,624,128]{2,1,0:T(8,128)(2,1)S(1)} %all_to_all.5.low_ref.high_ref.refs_0_.refs_1_.refs_2_.refs_3_.refs_4_.x_ref, s16[16,624,128]{2,1,0:T(8,128)(2,1)S(1)} %all_to_all.5.low_ref.high_ref.refs_0_.refs_1_.refs_2_.refs_3_.refs_4_.x_ref, ...), custom_call_target="tpu_custom_call", output_to_operand_aliasing={{}: (8, {})} | custom-call | tf_op jit(solution)/shard_map/outer/pallas_call | solution.py:370
  (1 shorter events, 0.0 us)
Async XLA Ops:
  2.0 2.4 %copy-start = (s32[2048]{0:T(1024)}, s32[2048]{0:T(1024)S(1)}, u32[]{:S(2)}) copy-start(s32[2048]{0:T(1024)S(1)} %get-tuple-element.12.base_ref) | copy-start | bytes 24580
  76.5 13.0 %collective-permute-start = (f32[8,2,512]{2,1,0:T(2,128)S(1)}, f32[8,2,512]{2,1,0:T(2,128)S(1)}, u32[]{:S(2)}, u32[]{:S(2)}) collective-permute-start(f32[8,2,512]{2,1,0:T(2,128)S(1)} %get-tuple-element.7), channel_id=1, source_target_pairs={{7,0},{0,1},{1,2},{2,3},{3,4},{4,5},{5,6},{6,7},{15,8},{8,9},{9,10... | collective-permute-start | bytes 98312 | tf_op jit(solution)/shard_map/ppermute | solution.py:293
  78.3 11.2 %collective-permute-start.1 = (f32[8,2,512]{2,1,0:T(2,128)S(1)}, f32[8,2,512]{2,1,0:T(2,128)S(1)}, u32[]{:S(2)}, u32[]{:S(2)}) collective-permute-start(f32[8,2,512]{2,1,0:T(2,128)S(1)} %get-tuple-element.8), channel_id=1, source_target_pairs={{1,0},{2,1},{3,2},{4,3},{5,4},{6,5},{7,6},{0,7},{9,8},{10,9},{11,1... | collective-permute-start | bytes 98312 | tf_op jit(solution)/shard_map/ppermute | solution.py:293

commit v4 on v3

v4 whole, which is shorter than its diff:
```python
import jax
import jax.numpy as jnp
import numpy as np
from jax import lax
from jax.experimental import pallas as pl
from jax.experimental.pallas import tpu as pltpu
from jax.sharding import PartitionSpec as P

NZ = 128
GROUP = 256
BATCH = 16
KZ = 16
UROWS = 24
VSLOTS = 34
FRONT = VSLOTS * UROWS
PLANE = UROWS * VSLOTS
GROWS = FRONT + 4 * KZ * PLANE
SPARE = -GROWS % 256 + 256
DUMP = GROWS + SPARE - 8
VOUT = 34
TAIL = VOUT * 16
SENT = TAIL + 80
WIRE = jnp.int16
LEVELS = 32700.0
UNROLL = 11
SCALE_ROW = TAIL + 34


def restriction():
    coef = [1.0, 4.0, 6.0, 4.0, 1.0]
    table = np.zeros((512, 384), np.float32)
    for p in range(8):
        for mm in range(6):
            tap = p + 4 - 2 * mm
            if not 0 <= tap < 5:
                continue
            for q in range(8):
                for r in range(8):
                    z, y = (r - 2) % 8, (q - 2) % 8
                    lane = z // 4 * 64 + mm % 2 * 32 + z % 4 * 8 + y
                    table[(p * 8 + q) * 8 + r, mm // 2 * 128 + lane] = coef[tap] / 8.0
    return np.concatenate([table, table], axis=0)


def place_blocks(shape_ref, box_ref, live, base_ref, fast_ref, flag_ref, code_ref):
    lane = lax.broadcasted_iota(jnp.int32, base_ref.shape, 1)
    slot = lax.broadcasted_iota(jnp.int32, base_ref.shape, 0) * 128 + lane
    box = box_ref[...]
    u = box >> 11
    v = (box >> 5) & 63
    w = box & 31
    kind = (w & 1) * 2 + (v & 1)
    base = FRONT + (kind * KZ + (w >> 1)) * PLANE + (v >> 1) * UROWS + 7 + u
    late = jnp.zeros(base.shape, jnp.int32)
    for d in range(1, BATCH):
        near = jnp.abs(base - pltpu.roll(base, d, 1)) < 3
        late = jnp.where(near & ((lane & (BATCH - 1)) >= d), 1, late)
    base_ref[...] = base
    fast_ref[...] = jnp.where(late == 1, DUMP, base)
    for d in (1, 2, 4, 8):
        late = late | pltpu.roll(late, 128 - d, 1)
    flag_ref[...] = late
    code = jnp.where(slot < live, shape_ref[...], 32) * 4 + kind
    code_ref[...] = code.astype(jnp.float32)


def spread_kernel(live_ref, q_ref, shape_ref, box_ref, w_any, r_any, out_ref, *scratch):
    grid_ref, w_ref, r_ref, pick_ref, half_a, half_b, kind_a, kind_b, tile_a, tile_b, plane_ref = scratch[:11]
    base_v, fast_v, flag_v, code_ref, base_ref, fast_ref, flag_ref, sems = scratch[11:]
    shapes_n = w_ref.shape[0] // 128
    copies = [pltpu.make_async_copy(w_any, w_ref, sems.at[0]), pltpu.make_async_copy(r_any, r_ref, sems.at[1])]
    for copy in copies:
        copy.start()
    place_blocks(shape_ref, box_ref, live_ref[0], base_v, fast_v, flag_v, code_ref)
    for i, (here, there) in enumerate(((base_v, base_ref), (fast_v, fast_ref), (flag_v, flag_ref))):
        copies.append(pltpu.make_async_copy(here, there, sems.at[2 + i]))
        copies[-1].start()
    for ref in (half_b, kind_b, tile_a):
        ref[...] = jnp.zeros(ref.shape, ref.dtype)

    def clear(step, carry):
        grid_ref[pl.ds(pl.multiple_of(step * 256, 256), 256), :] = jnp.zeros((256, 128), jnp.float32)
        return carry

    lax.fori_loop(0, (GROWS + SPARE) // 256, clear, 0)
    for copy in copies:
        copy.wait()

    def product(step, half_ref, kind_ref):
        begin = pl.multiple_of(step * GROUP, GROUP)
        qg = q_ref[pl.ds(begin, GROUP), :]
        codes = [code_ref[pl.ds(step * (GROUP // 128) + h, 1), :] for h in range(GROUP // 128)]
        code = jnp.concatenate([jnp.broadcast_to(c, (128, 128)).T for c in codes], axis=0)
        whole = jnp.floor(code * 0.25)
        sg = whole.astype(jnp.bfloat16)
        kind_ref[...] = code - 4.0 * whole
        for s in range(shapes_n):
            pick_ref[:, s * 128 : (s + 1) * 128] = jnp.where(sg == s, qg, jnp.zeros_like(qg))
        part = jnp.dot(pick_ref[...], w_ref[...], preferred_element_type=jnp.float32)
        high = part.astype(jnp.bfloat16)
        half_ref[:, :512] = high
        half_ref[:, 512:] = (part - high.astype(jnp.float32)).astype(jnp.bfloat16)

    def arrange(half_ref, kind_ref, tile_ref):
        cells = jnp.dot(half_ref[...], r_ref[...], preferred_element_type=jnp.float32)
        kind = kind_ref[...]
        z_odd = kind >= 2.0
        y_odd = (kind == 1.0) | (kind == 3.0)
        y_upper = (lax.broadcasted_iota(jnp.int32, kind.shape, 1) & 4) != 0
        for du in range(3):
            rows = cells[:, du * 128 : (du + 1) * 128]
            rows = jnp.where(z_odd, pltpu.roll(rows, 64, 1), rows)
            crossed = jnp.where(y_upper, pltpu.roll(rows, 4, 1), pltpu.roll(rows, 124, 1))
            tile_ref[pl.ds(du, GROUP, stride=4), :] = jnp.where(y_odd, crossed, rows)

    def at(ref, step, i):
        return ref[step * (GROUP // 128) + i // 128, i % 128]

    def deposit(step, tile_ref):
        for batch in range(GROUP // BATCH):
            slots = [batch * BATCH + j for j in range(BATCH)]
            rows = [at(fast_ref, step, i) for i in slots]
            sums = [grid_ref[pl.ds(r, 3), :] + tile_ref[4 * i : 4 * i + 3, :] for r, i in zip(rows, slots)]
            for r, value in zip(rows, sums):
                grid_ref[pl.ds(r, 3), :] = value

    def deposit_rest(step, tile_ref):
        flag = at(flag_ref, step, 0)
        for batch in range(1, GROUP // BATCH):
            flag = flag | at(flag_ref, step, batch * BATCH)

        @pl.when(flag != 0)
        def _():
            def one_batch(batch, carry):
                row = step * (GROUP // 128) + batch // (128 // BATCH)
                head = batch % (128 // BATCH) * BATCH

                @pl.when(flag_ref[row, head] != 0)
                def _():
                    def one_block(j, inner):
                        spot = base_ref[row, head + j]

                        @pl.when(fast_ref[row, head + j] != spot)
                        def _():
                            grid_ref[pl.ds(spot, 3), :] += tile_ref[pl.ds((batch * BATCH + j) * 4, 3), :]

                        return inner

                    lax.fori_loop(0, BATCH, one_block, 0)

                return carry

            lax.fori_loop(0, GROUP // BATCH, one_batch, 0)

    def two_groups(pair, carry):
        step = 2 * pair
        product(step, half_a, kind_a)
        arrange(half_b, kind_b, tile_b)
        deposit(jnp.maximum(step - 2, 0), tile_a)
        product(step + 1, half_b, kind_b)
        arrange(half_a, kind_a, tile_a)
        deposit(jnp.maximum(step - 1, 0), tile_b)

        @pl.when(pair > 0)
        def _():
            deposit_rest(step - 1, tile_b)

        deposit_rest(step, tile_a)
        return carry

    pairs = (live_ref[0] + 2 * GROUP - 1) // (2 * GROUP)
    lax.fori_loop(0, pairs, two_groups, 0)
    arrange(half_b, kind_b, tile_b)
    deposit(2 * pairs - 2, tile_a)
    deposit(2 * pairs - 1, tile_b)
    deposit_rest(2 * pairs - 1, tile_b)

    def one_plane(k, carry):
        combine(k, grid_ref, plane_ref, out_ref)
        return carry

    lax.fori_loop(0, KZ, one_plane, 0)


def combine(k, grid_ref, plane_ref, out_ref):
    lane = lax.broadcasted_iota(jnp.int32, (8, 128), 1)
    z = ((lane >> 6) << 2) + ((lane >> 3) & 3)
    z_kept = z < 6
    z_past = z < 2
    y_kept = (lane & 7) < 6
    y_past = (lane & 7) < 2
    next_k = lax.rem(k + 1, KZ)
    last_k = lax.rem(k + KZ - 1, KZ)

    def slab(odd, row):
        def at(copy, plane):
            return grid_ref[pl.ds(pl.multiple_of(FRONT + (copy * KZ + plane) * PLANE + row, 8), 8), :]

        return jnp.where(z_kept, at(odd, k), at(odd, next_k)) + jnp.where(z_past, at(2 + odd, last_k), at(2 + odd, k))

    def put(row, value, top):
        plane_ref[pl.ds(row, 8), :] = value
        return jnp.maximum(top, jnp.abs(value))

    def put_ends(v, value, top):
        plane_ref[pl.ds(TAIL + v, 1), :] = value[7:8]
        plane_ref[pl.ds(TAIL + 39 + v, 1), :] = value[0:1]
        return jnp.maximum(top, jnp.abs(value))

    def one_slab(v, carry):
        top, evens, odds = carry
        new_evens, new_odds = [], []
        for part in range(3):
            row = v * UROWS + 8 * part
            even, odd = slab(0, row), slab(1, row - UROWS)
            value = jnp.where(y_kept, evens[part], even) + jnp.where(y_past, odds[part], odd)
            if part == 0:
                top = put_ends(v, value, top)
            else:
                place = jnp.where(v == 0, VOUT - 2, v - 1)
                top = put(pl.multiple_of(place * 16 + 8 * part - 8, 8), value, top)
            new_evens.append(even)
            new_odds.append(odd)
        return top, tuple(new_evens), tuple(new_odds)

    zero = jnp.zeros((8, 128), jnp.float32)
    top, evens, odds = lax.fori_loop(0, VOUT - 1, one_slab, (zero, (zero,) * 3, (zero,) * 3), unroll=UNROLL)
    for part in (1, 2):
        top = put((VOUT - 1) * 16 + 8 * part - 8, jnp.where(y_past, odds[part], 0.0), top)
    odd = slab(1, 32 * UROWS)
    top = put_ends(33, jnp.where(y_kept, evens[0], 0.0) + jnp.where(y_past, odds[0], odd), top)
    value = jnp.where(y_past, odd, 0.0)
    plane_ref[TAIL + 73 : TAIL + 74, :] = value[0:1]
    top = jnp.maximum(top, jnp.abs(value))
    line = lax.broadcasted_iota(jnp.int32, (8, 128), 0)
    top = jnp.maximum(jnp.max(top, axis=0, keepdims=True), 1e-37)
    power = jnp.ceil(jnp.log2(top) * 16.0 + 0.01)
    shrink = jnp.exp2(power * -0.0625)
    last = plane_ref[SCALE_ROW - 2 : SCALE_ROW + 6, :]
    whole = jnp.round(plane_ref[...] * shrink * LEVELS)
    out_ref[k] = whole.astype(jnp.int32).astype(out_ref.dtype)
    marked = jnp.where(line == 2, power, jnp.round(last * shrink * LEVELS))
    both = jnp.concatenate([marked, jnp.round(plane_ref[SCALE_ROW + 6 : SCALE_ROW + 14, :] * shrink * LEVELS)], axis=0)
    out_ref[k, SCALE_ROW - 2 : SCALE_ROW + 14, :] = both.astype(jnp.int32).astype(out_ref.dtype)


def take_tails(tails, tail_ref, grow_ref):
    for src in range(16):
        tail = jnp.concatenate([t[src] for t in tails], axis=0).astype(jnp.float32)
        grow = jnp.exp2(tail[SCALE_ROW - TAIL : SCALE_ROW - TAIL + 1] * 0.0625) / LEVELS
        grow_ref[src * 8 : src * 8 + 8, :] = jnp.broadcast_to(grow, (8, 128))
        tail_ref[src * 80 : (src + 1) * 80, :] = tail * grow


def turn(rows_of, slabs, tail_ref, grow_ref, turn_ref):
    lane = lax.broadcasted_iota(jnp.int32, (8, 128), 1)
    line = lax.broadcasted_iota(jnp.int32, (8, 128), 0)
    for src in range(16):
        grow = grow_ref[src * 8 : src * 8 + 8, :]
        halves = []
        for which in range(2):
            both = rows_of(src, which).astype(jnp.float32)
            above = tail_ref[pl.ds((src + 1) % 16 * 80 + slabs[which], 1), :]
            below = tail_ref[pl.ds((src + 15) % 16 * 80 + 40 + slabs[which], 1), :]
            upper = both[0:8] * grow + jnp.where(line == 0, below, 0.0)
            lower = both[8:16] * grow + jnp.where(line == 7, above, 0.0)
            halves.append((upper, lower))
        for half in range(2):
            da, db = halves[0][half], halves[1][half]
            begin = src * 32 + half * 16
            turn_ref[pl.ds(begin, 8, stride=2), :] = jnp.where(lane & 32 == 0, da, pltpu.roll(db, 32, 1))
            turn_ref[pl.ds(begin + 1, 8, stride=2), :] = jnp.where(lane & 32 == 0, pltpu.roll(da, 96, 1), db)
    blocks = []
    for c in range(4):
        block = turn_ref[c * 128 : (c + 1) * 128, :].T.reshape(2, 2, 4, 8, 128)
        blocks.append([jnp.concatenate([block[0, which], block[1, which]], axis=0) for which in range(2)])
    return blocks


def edge_kernel(low_ref, high_ref, *refs):
    tails, (down_ref, up_ref), scratch = refs[:5], refs[5:7], refs[7:]
    take_tails(tails, *scratch[:2])
    blocks = turn(lambda src, which: (low_ref, high_ref)[which][src], (0, VOUT - 1), *scratch[:2], scratch[2].at[0])
    for c, block in enumerate(blocks):
        down_ref[:, :, c * 128 : (c + 1) * 128] = block[0][:, 6:8]
        up_ref[:, :, c * 128 : (c + 1) * 128] = block[1][:, 0:2]


def assemble(x_ref, first, out_ref, scratch):
    tail_ref, grow_ref, turn_refs = scratch
    for pair in range(2):
        rows_of = lambda src, which: x_ref[src, (2 * pair + which) * 16 : (2 * pair + which + 1) * 16, :]
        slabs = (first + 2 * pair, first + 2 * pair + 1)
        blocks = turn(rows_of, slabs, tail_ref, grow_ref, turn_refs.at[pair])
        for c, block in enumerate(blocks):
            for which in range(2):
                begin = pair * 16 + which * 8
                out_ref[:, begin : begin + 8, c * 128 : (c + 1) * 128] = block[which]


def inner_kernel(x_ref, *refs):
    tails, out_ref, scratch = refs[:5], refs[5], refs[6:]
    step = pl.program_id(0)

    @pl.when(step == 0)
    def _():
        take_tails(tails, *scratch[:2])

    assemble(x_ref, 4 * step + 5, out_ref, scratch)


def outer_kernel(x_ref, *refs):
    tails, (below_ref, above_ref, _, out_ref), scratch = refs[:5], refs[5:9], refs[9:]
    step = pl.program_id(0)

    @pl.when(step == 0)
    def _():
        take_tails(tails, *scratch[:2])

    assemble(x_ref, 28 * step + 1, out_ref, scratch)

    @pl.when(step == 0)
    def _():
        out_ref[:, 0:2, :] += below_ref[...]

    @pl.when(step == 1)
    def _():
        out_ref[:, 30:32, :] += above_ref[...]


def from_behind(block, axis, distance):
    devices = range(lax.axis_size(axis))
    route = [((i - distance) % len(devices), i) for i in devices]
    return lax.ppermute(block, axis, route)


def on_device(charges, weight_tiles, block_shape, block_box, live_blocks):
    nblk, atoms = charges.shape
    shapes_n, _, cells = weight_tiles.shape
    wflat = weight_tiles.reshape(shapes_n * atoms, cells)
    rows = (nblk // 128, 128)
    vmem = pl.BlockSpec(memory_space=pltpu.VMEM)
    smem = pl.BlockSpec(memory_space=pltpu.SMEM)
    hbm = pl.BlockSpec(memory_space=pl.ANY)
    sent = pl.pallas_call(
        spread_kernel,
        out_shape=jax.ShapeDtypeStruct((KZ, SENT, 128), WIRE),
        in_specs=[smem] + [vmem] * 3 + [hbm] * 2,
        out_specs=vmem,
        scratch_shapes=[
            pltpu.VMEM((GROWS + SPARE, 128), jnp.float32),
            pltpu.VMEM((shapes_n * atoms, cells), jnp.bfloat16),
            pltpu.VMEM((1024, 384), jnp.bfloat16),
            pltpu.VMEM((GROUP, shapes_n * atoms), jnp.bfloat16),
            pltpu.VMEM((GROUP, 1024), jnp.bfloat16),
            pltpu.VMEM((GROUP, 1024), jnp.bfloat16),
            pltpu.VMEM((GROUP, 128), jnp.float32),
            pltpu.VMEM((GROUP, 128), jnp.float32),
            pltpu.VMEM((GROUP * 4, 128), jnp.float32),
            pltpu.VMEM((GROUP * 4, 128), jnp.float32),
            pltpu.VMEM((SENT, 128), jnp.float32),
            pltpu.VMEM(rows, jnp.int32),
            pltpu.VMEM(rows, jnp.int32),
            pltpu.VMEM(rows, jnp.int32),
            pltpu.VMEM(rows, jnp.float32),
            pltpu.SMEM(rows, jnp.int32),
            pltpu.SMEM(rows, jnp.int32),
            pltpu.SMEM(rows, jnp.int32),
            pltpu.SemaphoreType.DMA((5,)),
        ],
        compiler_params=pltpu.CompilerParams(vmem_limit_bytes=56 * 1024 * 1024),
        name="spread",
    )(
        live_blocks,
        charges,
        block_shape.reshape(rows),
        block_box.reshape(rows),
        wflat,
        jnp.asarray(restriction(), jnp.bfloat16),
    )
    got = lax.all_to_all(sent, "bx", split_axis=0, concat_axis=0, tiled=True)
    piece = lambda i: pl.BlockSpec((KZ, 16, 128), lambda p: (0, i, 0))
    tails = [piece(TAIL // 16 + i) for i in range(5)]
    small = pl.BlockSpec((8, 2, 512), lambda p: (0, 0, 0))
    full = jax.ShapeDtypeStruct((8, 256, 512), jnp.float32)
    scratch = [
        pltpu.VMEM((16 * 80, 128), jnp.float32),
        pltpu.VMEM((128, 128), jnp.float32),
        pltpu.VMEM((2, 512, 128), jnp.float32),
    ]
    params = pltpu.CompilerParams(vmem_limit_bytes=40 * 1024 * 1024)
    down, up = pl.pallas_call(
        edge_kernel,
        out_shape=(jax.ShapeDtypeStruct((8, 2, 512), jnp.float32),) * 2,
        grid=(1,),
        in_specs=[piece(VOUT - 2), piece(VOUT - 1)] + tails,
        out_specs=(small, small),
        scratch_shapes=scratch,
        compiler_params=params,
        name="edge",
    )(*[got] * 7)
    below = from_behind(up, "by", 1)
    above = from_behind(down, "by", -1)
    inner = pl.pallas_call(
        inner_kernel,
        out_shape=full,
        grid=(6,),
        in_specs=[pl.BlockSpec((KZ, 64, 128), lambda p: (0, p + 1, 0))] + tails,
        out_specs=pl.BlockSpec((8, 32, 512), lambda p: (0, p + 1, 0)),
        scratch_shapes=scratch,
        compiler_params=params,
        name="inner",
    )(*[got] * 6)
    return pl.pallas_call(
        outer_kernel,
        out_shape=full,
        grid=(2,),
        in_specs=[pl.BlockSpec((KZ, 64, 128), lambda p: (0, 7 * p, 0))]
        + tails
        + [small, small, pl.BlockSpec(memory_space=pl.ANY)],
        out_specs=pl.BlockSpec((8, 32, 512), lambda p: (0, 7 * p, 0)),
        scratch_shapes=scratch,
        input_output_aliases={8: 0},
        compiler_params=params,
        name="outer",
    )(*[got] * 6, below, above, inner)


def solution(mesh):
    return jax.shard_map(
        on_device,
        mesh=mesh,
        in_specs=(P(("bx", "by"), None), P(), P(("bx", "by")), P(("bx", "by")), P(("bx", "by"))),
        out_specs=P("bx", "by", None),
        check_vma=False,
    )
```

time: 90.7 us -> 81 us (0.89); the launches traced: 91 us -> 79.9 us
  blocking collectives: 41.5 us -> 37.1 us
  Pallas kernels: 39.5 us -> 36.4 us
  other arithmetic: 2.69 us -> 0 us
  local copies, waits for them, and re-layouts: 0.98 us -> 0 us
    all_to_all x1, blocking collectives: 41.5 us -> 37.1 us  [on_device(): got = lax.all_to_all(sent, 'bx', split_axis=0, concat_axis=0, tiled=True)]
    pallas_call x1, Pallas kernels: 7.33 us -> 4.27 us  [on_device(): pl.pallas_call(inner_kernel, out_shape=full, grid=(6,), in_specs=[pl.Bloc...]
    reshape x1 -> x0, other arithmetic: 1.34 us -> none  [on_device(): code = code.astype(jnp.float32).reshape(nblk // 128, 128)]
  transfers between devices with their start and end apart: 2 -> 2, of which waited for: 0 -> 0; matrix products, arithmetic and copies ran while one was open for 0% -> 0% of each run, Pallas kernels for 8% -> 5%
where the time goes in v4:
time: 81 us; the launch traced here: 79.9 us
  blocking collectives  37.1 us (46%)
  Pallas kernels  36.4 us (45%)
  starting transfers between devices  5.71 us (7%)
    all_to_all x1, blocking collectives, on_device(): got = lax.all_to_all(sent, 'bx', split_axis=0, concat_axis=0, tiled=True)  37.1 us
    pallas_call x1, Pallas kernels, on_device(): pl.pallas_call(spread_kernel, out_shape=jax.ShapeDtypeStruct((KZ, SENT, 1...  30 us
    ppermute x2, starting transfers between devices, from_behind(): return lax.ppermute(block, axis, route)  5.71 us
    pallas_call x1, Pallas kernels, on_device(): pl.pallas_call(inner_kernel, out_shape=full, grid=(6,), in_specs=[pl.Bloc...  4.27 us
    pallas_call x1, Pallas kernels, on_device(): pl.pallas_call(outer_kernel, out_shape=full, grid=(2,), in_specs=[pl.Bloc...  1.86 us
  transfers between devices with their start and end apart: 2, of which 0 were waited for; matrix products, arithmetic and copies ran while one was open for 0% of the time, Pallas kernels for 5%

profile of v4, /device:TPU:0, one launch (start us, length us, event | category | flops | bytes accessed | tf_op | source)
XLA Modules:
  0.0 79.9 jit_solution(14687742640137117312)
XLA Ops:
  0.7 30.0 %spread.1 = s16[16,624,128]{2,1,0:T(8,128)(2,1)} custom-call(s32[1]{0:T(128)S(6)} %copy.9.live_ref, bf16[2048,128]{1,0:T(8,128)(2,1)} %q_ref.1, s32[16,128]{1,0:T(8,128)} %bitcast.4, s32[16,128]{1,0:T(8,128)} %bitcast.5, bf16[4096,512]{1,0:T(8,128)(2,1)} %bitcast.3, bf16[1024,384]{1,0:T(8,128)(2,1)} %constant.2.clone.r_any), custom_call_target="tpu_custom_call" | custom-call | tf_op jit(solution)/shard_map/spread/pallas_call | solution.py:345
  30.6 37.1 %all_to_all.5.low_ref.high_ref.refs_0_.refs_1_.refs_2_.refs_3_.refs_4_.x_ref = s16[16,624,128]{2,1,0:T(8,128)(2,1)S(1)} all-to-all(s16[16,624,128]{2,1,0:T(8,128)(2,1)} %spread.1), channel_id=1, replica_groups=mesh['bx'=16,'by'=8] {'bx'}, dimensions={0} | all-to-all | bytes 5111808 | tf_op jit(solution)/shard_map/all_to_all | solution.py:381
  67.7 0.3 edge.1
  68.0 4.5 %collective-permute-start = (f32[8,2,512]{2,1,0:T(2,128)S(1)}, f32[8,2,512]{2,1,0:T(2,128)S(1)}, u32[]{:S(2)}, u32[]{:S(2)}) collective-permute-start(f32[8,2,512]{2,1,0:T(2,128)S(1)} %get-tuple-element.7), channel_id=1, source_target_pairs={{7,0},{0,1},{1,2},{2,3},{3,4},{4,5},{5,6},{6,7},{15,8},{8,9},{9,10... | collective-permute-start | bytes 98312 | tf_op jit(solution)/shard_map/ppermute | solution.py:334
  72.6 1.2 %collective-permute-start.1 = (f32[8,2,512]{2,1,0:T(2,128)S(1)}, f32[8,2,512]{2,1,0:T(2,128)S(1)}, u32[]{:S(2)}, u32[]{:S(2)}) collective-permute-start(f32[8,2,512]{2,1,0:T(2,128)S(1)} %get-tuple-element.8), channel_id=1, source_target_pairs={{1,0},{2,1},{3,2},{4,3},{5,4},{6,5},{7,6},{0,7},{9,8},{10,9},{11,1... | collective-permute-start | bytes 98312 | tf_op jit(solution)/shard_map/ppermute | solution.py:334
  73.8 4.3 %inner.1.refs_7_ = f32[8,256,512]{2,1,0:T(8,128)} custom-call(s16[16,624,128]{2,1,0:T(8,128)(2,1)S(1)} %all_to_all.5.low_ref.high_ref.refs_0_.refs_1_.refs_2_.refs_3_.refs_4_.x_ref, s16[16,624,128]{2,1,0:T(8,128)(2,1)S(1)} %all_to_all.5.low_ref.high_ref.refs_0_.refs_1_.refs_2_.refs_3_.refs_4_.x_ref, ...), custom_call_target="tpu_custom_call" | custom-call | tf_op jit(solution)/shard_map/inner/pallas_call | solution.py:404
  78.0 0.0 collective-permute-done.refs_5_
  78.0 0.0 collective-permute-done.1.refs_6_
  78.0 1.9 %outer.1 = f32[8,256,512]{2,1,0:T(8,128)} custom-call(s16[16,624,128]{2,1,0:T(8,128)(2,1)S(1)} %all_to_all.5.low_ref.high_ref.refs_0_.refs_1_.refs_2_.refs_3_.refs_4_.x_ref, s16[16,624,128]{2,1,0:T(8,128)(2,1)S(1)} %all_to_all.5.low_ref.high_ref.refs_0_.refs_1_.refs_2_.refs_3_.refs_4_.x_ref, ...), custom_call_target="tpu_custom_call", output_to_operand_aliasing={{}: (8, {})} | custom-call | tf_op jit(solution)/shard_map/outer/pallas_call | solution.py:414
Async XLA Ops:
  68.0 10.0 %collective-permute-start = (f32[8,2,512]{2,1,0:T(2,128)S(1)}, f32[8,2,512]{2,1,0:T(2,128)S(1)}, u32[]{:S(2)}, u32[]{:S(2)}) collective-permute-start(f32[8,2,512]{2,1,0:T(2,128)S(1)} %get-tuple-element.7), channel_id=1, source_target_pairs={{7,0},{0,1},{1,2},{2,3},{3,4},{4,5},{5,6},{6,7},{15,8},{8,9},{9,10... | collective-permute-start | bytes 98312 | tf_op jit(solution)/shard_map/ppermute | solution.py:334
  72.6 5.4 %collective-permute-start.1 = (f32[8,2,512]{2,1,0:T(2,128)S(1)}, f32[8,2,512]{2,1,0:T(2,128)S(1)}, u32[]{:S(2)}, u32[]{:S(2)}) collective-permute-start(f32[8,2,512]{2,1,0:T(2,128)S(1)} %get-tuple-element.8), channel_id=1, source_target_pairs={{1,0},{2,1},{3,2},{4,3},{5,4},{6,5},{7,6},{0,7},{9,8},{10,9},{11,1... | collective-permute-start | bytes 98312 | tf_op jit(solution)/shard_map/ppermute | solution.py:334

commit v5 on v4

--- a/solution.py
+++ b/solution.py
@@ -17,13 +17,13 @@
 GROWS = FRONT + 4 * KZ * PLANE
 SPARE = -GROWS % 256 + 256
 DUMP = GROWS + SPARE - 8
-VOUT = 34
-TAIL = VOUT * 16
+EDGE = 512
+TAIL = EDGE + 16
 SENT = TAIL + 80
 WIRE = jnp.int16
 LEVELS = 32700.0
 UNROLL = 11
-SCALE_ROW = TAIL + 34
+SCALE_ROW = TAIL + 33
 
 
 def restriction():
@@ -64,9 +64,9 @@
     code_ref[...] = code.astype(jnp.float32)
 
 
-def spread_kernel(live_ref, q_ref, shape_ref, box_ref, w_any, r_any, out_ref, *scratch):
+def spread_kernel(live_ref, q_ref, shape_ref, box_ref, w_any, r_any, out_any, *scratch):
     grid_ref, w_ref, r_ref, pick_ref, half_a, half_b, kind_a, kind_b, tile_a, tile_b, plane_ref = scratch[:11]
-    base_v, fast_v, flag_v, code_ref, base_ref, fast_ref, flag_ref, sems = scratch[11:]
+    base_v, fast_v, flag_v, code_ref, base_ref, fast_ref, flag_ref, out_ref, sems, out_sems = scratch[11:]
     shapes_n = w_ref.shape[0] // 128
     copies = [pltpu.make_async_copy(w_any, w_ref, sems.at[0]), pltpu.make_async_copy(r_any, r_ref, sems.at[1])]
     for copy in copies:
@@ -94,9 +94,10 @@
         whole = jnp.floor(code * 0.25)
         sg = whole.astype(jnp.bfloat16)
         kind_ref[...] = code - 4.0 * whole
-        for s in range(shapes_n):
-            pick_ref[:, s * 128 : (s + 1) * 128] = jnp.where(sg == s, qg, jnp.zeros_like(qg))
-        part = jnp.dot(pick_ref[...], w_ref[...], preferred_element_type=jnp.float32)
+        part = jnp.zeros((GROUP, 512), jnp.float32)
+        for s in range(0, shapes_n, 2):
+            pick = jnp.concatenate([jnp.where(sg == s + i, qg, jnp.zeros_like(qg)) for i in range(2)], axis=1)
+            part += jnp.dot(pick, w_ref[s * 128 : (s + 2) * 128, :], preferred_element_type=jnp.float32)
         high = part.astype(jnp.bfloat16)
         half_ref[:, :512] = high
         half_ref[:, 512:] = (part - high.astype(jnp.float32)).astype(jnp.bfloat16)
@@ -154,11 +155,11 @@
 
     def two_groups(pair, carry):
         step = 2 * pair
+        arrange(half_b, kind_b, tile_b)
         product(step, half_a, kind_a)
-        arrange(half_b, kind_b, tile_b)
         deposit(jnp.maximum(step - 2, 0), tile_a)
+        arrange(half_a, kind_a, tile_a)
         product(step + 1, half_b, kind_b)
-        arrange(half_a, kind_a, tile_a)
         deposit(jnp.maximum(step - 1, 0), tile_b)
 
         @pl.when(pair > 0)
@@ -175,73 +176,88 @@
     deposit(2 * pairs - 1, tile_b)
     deposit_rest(2 * pairs - 1, tile_b)
 
-    def one_plane(k, carry):
-        combine(k, grid_ref, plane_ref, out_ref)
+    def out_copy(k):
+        return pltpu.make_async_copy(out_ref.at[k], out_any.at[k], out_sems.at[k])
+
+    def two_planes(pair, carry):
+        combine(2 * pair, grid_ref, plane_ref)
+        for i in range(2):
+            encode(plane_ref.at[i], out_ref.at[2 * pair + i])
+            out_copy(2 * pair + i).start()
         return carry
 
-    lax.fori_loop(0, KZ, one_plane, 0)
-
-
-def combine(k, grid_ref, plane_ref, out_ref):
+    lax.fori_loop(0, KZ // 2, two_planes, 0)
+    for k in range(KZ):
+        out_copy(k).wait()
+
+
+def combine(k, grid_ref, plane_ref):
     lane = lax.broadcasted_iota(jnp.int32, (8, 128), 1)
     z = ((lane >> 6) << 2) + ((lane >> 3) & 3)
     z_kept = z < 6
     z_past = z < 2
     y_kept = (lane & 7) < 6
     y_past = (lane & 7) < 2
-    next_k = lax.rem(k + 1, KZ)
     last_k = lax.rem(k + KZ - 1, KZ)
-
-    def slab(odd, row):
+    third_k = lax.rem(k + 2, KZ)
+
+    def slabs(odd, row):
         def at(copy, plane):
             return grid_ref[pl.ds(pl.multiple_of(FRONT + (copy * KZ + plane) * PLANE + row, 8), 8), :]
 
-        return jnp.where(z_kept, at(odd, k), at(odd, next_k)) + jnp.where(z_past, at(2 + odd, last_k), at(2 + odd, k))
-
-    def put(row, value, top):
-        plane_ref[pl.ds(row, 8), :] = value
-        return jnp.maximum(top, jnp.abs(value))
-
-    def put_ends(v, value, top):
-        plane_ref[pl.ds(TAIL + v, 1), :] = value[7:8]
-        plane_ref[pl.ds(TAIL + 39 + v, 1), :] = value[0:1]
-        return jnp.maximum(top, jnp.abs(value))
+        even = [at(odd, p) for p in (k, k + 1, third_k)]
+        odd = [at(2 + odd, p) for p in (last_k, k, k + 1)]
+        return [jnp.where(z_kept, even[i], even[i + 1]) + jnp.where(z_past, odd[i], odd[i + 1]) for i in range(2)]
+
+    def put_ends(i, below, above, value):
+        plane_ref[i, pl.ds(TAIL + below, 1), :] = value[7:8]
+        plane_ref[i, pl.ds(TAIL + 40 + above, 1), :] = value[0:1]
 
     def one_slab(v, carry):
-        top, evens, odds = carry
+        evens, odds = carry
+        place = jnp.where(v == 0, 32, v - 1)
+        above = jnp.where(v < 2, 33 - v, v - 2)
         new_evens, new_odds = [], []
         for part in range(3):
             row = v * UROWS + 8 * part
-            even, odd = slab(0, row), slab(1, row - UROWS)
-            value = jnp.where(y_kept, evens[part], even) + jnp.where(y_past, odds[part], odd)
-            if part == 0:
-                top = put_ends(v, value, top)
-            else:
-                place = jnp.where(v == 0, VOUT - 2, v - 1)
-                top = put(pl.multiple_of(place * 16 + 8 * part - 8, 8), value, top)
+            even, odd = slabs(0, row), slabs(1, row - UROWS)
+            for i in range(2):
+                value = jnp.where(y_kept, evens[part][i], even[i]) + jnp.where(y_past, odds[part][i], odd[i])
+                if part == 0:
+                    put_ends(i, place, above, value)
+                else:
+                    plane_ref[i, pl.ds(pl.multiple_of(place * 16 + 8 * part - 8, 8), 8), :] = value
             new_evens.append(even)
             new_odds.append(odd)
-        return top, tuple(new_evens), tuple(new_odds)
+        return new_evens, new_odds
 
     zero = jnp.zeros((8, 128), jnp.float32)
-    top, evens, odds = lax.fori_loop(0, VOUT - 1, one_slab, (zero, (zero,) * 3, (zero,) * 3), unroll=UNROLL)
-    for part in (1, 2):
-        top = put((VOUT - 1) * 16 + 8 * part - 8, jnp.where(y_past, odds[part], 0.0), top)
-    odd = slab(1, 32 * UROWS)
-    top = put_ends(33, jnp.where(y_kept, evens[0], 0.0) + jnp.where(y_past, odds[0], odd), top)
-    value = jnp.where(y_past, odd, 0.0)
-    plane_ref[TAIL + 73 : TAIL + 74, :] = value[0:1]
-    top = jnp.maximum(top, jnp.abs(value))
+    start = [[zero] * 2] * 3
+    evens, odds = lax.fori_loop(0, 33, one_slab, (start, start), unroll=UNROLL)
+    odd = slabs(1, 32 * UROWS)
+    for i in range(2):
+        for part in (1, 2):
+            begin = EDGE + 8 * part - 8
+            plane_ref[i, begin : begin + 8, :] += jnp.where(y_past, odds[part][i], 0.0)
+        value = jnp.where(y_kept, evens[0][i], 0.0) + jnp.where(y_past, odds[0][i], odd[i])
+        plane_ref[i, TAIL + 32 : TAIL + 33, :] += value[7:8]
+        plane_ref[i, TAIL + 71 : TAIL + 72, :] = value[0:1]
+        plane_ref[i, TAIL + 72 : TAIL + 73, :] += jnp.where(y_past, odd[i], 0.0)[0:1]
+
+
+def encode(plane_ref, out_ref):
     line = lax.broadcasted_iota(jnp.int32, (8, 128), 0)
-    top = jnp.maximum(jnp.max(top, axis=0, keepdims=True), 1e-37)
-    power = jnp.ceil(jnp.log2(top) * 16.0 + 0.01)
+    top = jnp.max(jnp.abs(plane_ref[: TAIL + 33, :]), axis=0, keepdims=True)
+    top = jnp.maximum(top, jnp.max(jnp.abs(plane_ref[TAIL + 40 : TAIL + 73, :]), axis=0, keepdims=True))
+    power = jnp.ceil(jnp.log2(jnp.maximum(top, 1e-37)) * 16.0 + 0.01)
     shrink = jnp.exp2(power * -0.0625)
-    last = plane_ref[SCALE_ROW - 2 : SCALE_ROW + 6, :]
     whole = jnp.round(plane_ref[...] * shrink * LEVELS)
-    out_ref[k] = whole.astype(jnp.int32).astype(out_ref.dtype)
-    marked = jnp.where(line == 2, power, jnp.round(last * shrink * LEVELS))
-    both = jnp.concatenate([marked, jnp.round(plane_ref[SCALE_ROW + 6 : SCALE_ROW + 14, :] * shrink * LEVELS)], axis=0)
-    out_ref[k, SCALE_ROW - 2 : SCALE_ROW + 14, :] = both.astype(jnp.int32).astype(out_ref.dtype)
+    out_ref[...] = whole.astype(jnp.int32).astype(out_ref.dtype)
+    begin = SCALE_ROW // 16 * 16
+    marked = jnp.round(plane_ref[begin : begin + 8, :] * shrink * LEVELS)
+    marked = jnp.where(line == SCALE_ROW - begin, power, marked)
+    rest = jnp.round(plane_ref[begin + 8 : begin + 16, :] * shrink * LEVELS)
+    out_ref[begin : begin + 16, :] = jnp.concatenate([marked, rest], axis=0).astype(jnp.int32).astype(out_ref.dtype)
 
 
 def take_tails(tails, tail_ref, grow_ref):
@@ -258,13 +274,15 @@
     for src in range(16):
         grow = grow_ref[src * 8 : src * 8 + 8, :]
         halves = []
-        for which in range(2):
+        for which in range(len(slabs)):
             both = rows_of(src, which).astype(jnp.float32)
             above = tail_ref[pl.ds((src + 1) % 16 * 80 + slabs[which], 1), :]
             below = tail_ref[pl.ds((src + 15) % 16 * 80 + 40 + slabs[which], 1), :]
             upper = both[0:8] * grow + jnp.where(line == 0, below, 0.0)
             lower = both[8:16] * grow + jnp.where(line == 7, above, 0.0)
             halves.append((upper, lower))
+        if len(slabs) == 1:
+            halves.append((jnp.zeros((8, 128), jnp.float32),) * 2)
         for half in range(2):
             da, db = halves[0][half], halves[1][half]
             begin = src * 32 + half * 16
@@ -277,13 +295,13 @@
     return blocks
 
 
-def edge_kernel(low_ref, high_ref, *refs):
+def edge_kernel(x_ref, *refs):
     tails, (down_ref, up_ref), scratch = refs[:5], refs[5:7], refs[7:]
     take_tails(tails, *scratch[:2])
-    blocks = turn(lambda src, which: (low_ref, high_ref)[which][src], (0, VOUT - 1), *scratch[:2], scratch[2].at[0])
+    blocks = turn(lambda src, which: x_ref[src], (32,), *scratch[:2], scratch[2].at[0])
     for c, block in enumerate(blocks):
         down_ref[:, :, c * 128 : (c + 1) * 128] = block[0][:, 6:8]
-        up_ref[:, :, c * 128 : (c + 1) * 128] = block[1][:, 0:2]
+        up_ref[:, :, c * 128 : (c + 1) * 128] = block[0][:, 0:2]
 
 
 def assemble(x_ref, first, out_ref, scratch):
@@ -306,7 +324,7 @@
     def _():
         take_tails(tails, *scratch[:2])
 
-    assemble(x_ref, 4 * step + 5, out_ref, scratch)
+    assemble(x_ref, 4 * step + 4, out_ref, scratch)
 
 
 def outer_kernel(x_ref, *refs):
@@ -317,7 +335,7 @@
     def _():
         take_tails(tails, *scratch[:2])
 
-    assemble(x_ref, 28 * step + 1, out_ref, scratch)
+    assemble(x_ref, 28 * step, out_ref, scratch)
 
     @pl.when(step == 0)
     def _():
@@ -346,7 +364,7 @@
         spread_kernel,
         out_shape=jax.ShapeDtypeStruct((KZ, SENT, 128), WIRE),
         in_specs=[smem] + [vmem] * 3 + [hbm] * 2,
-        out_specs=vmem,
+        out_specs=hbm,
         scratch_shapes=[
             pltpu.VMEM((GROWS + SPARE, 128), jnp.float32),
             pltpu.VMEM((shapes_n * atoms, cells), jnp.bfloat16),
@@ -358,7 +376,7 @@
             pltpu.VMEM((GROUP, 128), jnp.float32),
             pltpu.VMEM((GROUP * 4, 128), jnp.float32),
             pltpu.VMEM((GROUP * 4, 128), jnp.float32),
-            pltpu.VMEM((SENT, 128), jnp.float32),
+            pltpu.VMEM((2, SENT, 128), jnp.float32),
             pltpu.VMEM(rows, jnp.int32),
             pltpu.VMEM(rows, jnp.int32),
             pltpu.VMEM(rows, jnp.int32),
@@ -366,7 +384,9 @@
             pltpu.SMEM(rows, jnp.int32),
             pltpu.SMEM(rows, jnp.int32),
             pltpu.SMEM(rows, jnp.int32),
+            pltpu.VMEM((KZ, SENT, 128), WIRE),
             pltpu.SemaphoreType.DMA((5,)),
+            pltpu.SemaphoreType.DMA((KZ,)),
         ],
         compiler_params=pltpu.CompilerParams(vmem_limit_bytes=56 * 1024 * 1024),
         name="spread",
@@ -393,12 +413,12 @@
         edge_kernel,
         out_shape=(jax.ShapeDtypeStruct((8, 2, 512), jnp.float32),) * 2,
         grid=(1,),
-        in_specs=[piece(VOUT - 2), piece(VOUT - 1)] + tails,
+        in_specs=[piece(EDGE // 16)] + tails,
         out_specs=(small, small),
         scratch_shapes=scratch,
         compiler_params=params,
         name="edge",
-    )(*[got] * 7)
+    )(*[got] * 6)
     below = from_behind(up, "by", 1)
     above = from_behind(down, "by", -1)
     inner = pl.pallas_call(

time: 81 us -> 75.4 us (0.931)
  Pallas kernels: 36.4 us -> 19.2 us
  blocking collectives: 37.1 us -> 49.3 us
    pallas_call x1, Pallas kernels: 30 us -> 12.8 us  [on_device(): pl.pallas_call(spread_kernel, out_shape=jax.ShapeDtypeStruct((KZ, SENT, 1...]
    all_to_all x1, blocking collectives: 37.1 us -> 49.3 us  [on_device(): got = lax.all_to_all(sent, 'bx', split_axis=0, concat_axis=0, tiled=True)]
  transfers between devices with their start and end apart: 2 -> 2, of which waited for: 0 -> 0; matrix products, arithmetic and copies ran while one was open for 0% -> 0% of each run, Pallas kernels for 5% -> 6%
where the time goes in v5:
time: 75.4 us; the launch traced here: 74.9 us
  blocking collectives  49.3 us (65%)
  Pallas kernels  19.2 us (25%)
  starting transfers between devices  5.79 us (8%)
    all_to_all x1, blocking collectives, on_device(): got = lax.all_to_all(sent, 'bx', split_axis=0, concat_axis=0, tiled=True)  49.3 us
    pallas_call x1, Pallas kernels, on_device(): pl.pallas_call(spread_kernel, out_shape=jax.ShapeDtypeStruct((KZ, SENT, 1...  12.8 us
    ppermute x2, starting transfers between devices, from_behind(): return lax.ppermute(block, axis, route)  5.79 us
    pallas_call x1, Pallas kernels, on_device(): pl.pallas_call(inner_kernel, out_shape=full, grid=(6,), in_specs=[pl.Bloc...  4.27 us
    pallas_call x1, Pallas kernels, on_device(): pl.pallas_call(outer_kernel, out_shape=full, grid=(2,), in_specs=[pl.Bloc...  1.86 us
  transfers between devices with their start and end apart: 2, of which 0 were waited for; matrix products, arithmetic and copies ran while one was open for 0% of the time, Pallas kernels for 6%

profile of v5, /device:TPU:0, one launch (start us, length us, event | category | flops | bytes accessed | tf_op | source)
XLA Modules:
  0.0 74.9 jit_solution(16889874416014450146)
XLA Ops:
  0.7 12.8 %spread.1 = s16[16,608,128]{2,1,0:T(8,128)(2,1)} custom-call(s32[1]{0:T(128)S(6)} %copy.9.live_ref, bf16[2048,128]{1,0:T(8,128)(2,1)} %q_ref.1, s32[16,128]{1,0:T(8,128)} %bitcast.4, s32[16,128]{1,0:T(8,128)} %bitcast.5, bf16[4096,512]{1,0:T(8,128)(2,1)} %bitcast.3, bf16[1024,384]{1,0:T(8,128)(2,1)} %constant.2.clone.r_any), custom_call_target="tpu_custom_call" | custom-call | tf_op jit(solution)/shard_map/spread/pallas_call | solution.py:363
  13.5 49.3 %all_to_all.5.x_ref.refs_0_.refs_1_.refs_2_.refs_3_.refs_4_ = s16[16,608,128]{2,1,0:T(8,128)(2,1)S(1)} all-to-all(s16[16,608,128]{2,1,0:T(8,128)(2,1)} %spread.1), channel_id=1, replica_groups=mesh['bx'=16,'by'=8] {'bx'}, dimensions={0} | all-to-all | bytes 4980736 | tf_op jit(solution)/shard_map/all_to_all | solution.py:401
  62.7 0.3 edge.1
  63.0 2.4 %collective-permute-start = (f32[8,2,512]{2,1,0:T(2,128)S(1)}, f32[8,2,512]{2,1,0:T(2,128)S(1)}, u32[]{:S(2)}, u32[]{:S(2)}) collective-permute-start(f32[8,2,512]{2,1,0:T(2,128)S(1)} %get-tuple-element.7), channel_id=1, source_target_pairs={{7,0},{0,1},{1,2},{2,3},{3,4},{4,5},{5,6},{6,7},{15,8},{8,9},{9,10... | collective-permute-start | bytes 98312 | tf_op jit(solution)/shard_map/ppermute | solution.py:352
  65.5 3.3 %collective-permute-start.1 = (f32[8,2,512]{2,1,0:T(2,128)S(1)}, f32[8,2,512]{2,1,0:T(2,128)S(1)}, u32[]{:S(2)}, u32[]{:S(2)}) collective-permute-start(f32[8,2,512]{2,1,0:T(2,128)S(1)} %get-tuple-element.8), channel_id=1, source_target_pairs={{1,0},{2,1},{3,2},{4,3},{5,4},{6,5},{7,6},{0,7},{9,8},{10,9},{11,1... | collective-permute-start | bytes 98312 | tf_op jit(solution)/shard_map/ppermute | solution.py:352
  68.8 4.3 %inner.1.refs_7_ = f32[8,256,512]{2,1,0:T(8,128)} custom-call(s16[16,608,128]{2,1,0:T(8,128)(2,1)S(1)} %all_to_all.5.x_ref.refs_0_.refs_1_.refs_2_.refs_3_.refs_4_, s16[16,608,128]{2,1,0:T(8,128)(2,1)S(1)} %all_to_all.5.x_ref.refs_0_.refs_1_.refs_2_.refs_3_.refs_4_, s16[16,608,128]{2,1,0:T(8,128)(2,1)S(1)} %all_to_all.5.x_ref.refs_0_.refs_1_.refs_2_.refs_3_.refs_4_, ...), custom_call_target="tpu_custom_call" | custom-call | tf_op jit(solution)/shard_map/inner/pallas_call | solution.py:424
  73.1 0.0 collective-permute-done.refs_5_
  73.1 0.0 collective-permute-done.1.refs_6_
  73.1 1.9 %outer.1 = f32[8,256,512]{2,1,0:T(8,128)} custom-call(s16[16,608,128]{2,1,0:T(8,128)(2,1)S(1)} %all_to_all.5.x_ref.refs_0_.refs_1_.refs_2_.refs_3_.refs_4_, s16[16,608,128]{2,1,0:T(8,128)(2,1)S(1)} %all_to_all.5.x_ref.refs_0_.refs_1_.refs_2_.refs_3_.refs_4_, ...), custom_call_target="tpu_custom_call", output_to_operand_aliasing={{}: (8, {})} | custom-call | tf_op jit(solution)/shard_map/outer/pallas_call | solution.py:434
Async XLA Ops:
  63.0 10.1 %collective-permute-start = (f32[8,2,512]{2,1,0:T(2,128)S(1)}, f32[8,2,512]{2,1,0:T(2,128)S(1)}, u32[]{:S(2)}, u32[]{:S(2)}) collective-permute-start(f32[8,2,512]{2,1,0:T(2,128)S(1)} %get-tuple-element.7), channel_id=1, source_target_pairs={{7,0},{0,1},{1,2},{2,3},{3,4},{4,5},{5,6},{6,7},{15,8},{8,9},{9,10... | collective-permute-start | bytes 98312 | tf_op jit(solution)/shard_map/ppermute | solution.py:352
  65.5 7.6 %collective-permute-start.1 = (f32[8,2,512]{2,1,0:T(2,128)S(1)}, f32[8,2,512]{2,1,0:T(2,128)S(1)}, u32[]{:S(2)}, u32[]{:S(2)}) collective-permute-start(f32[8,2,512]{2,1,0:T(2,128)S(1)} %get-tuple-element.8), channel_id=1, source_target_pairs={{1,0},{2,1},{3,2},{4,3},{5,4},{6,5},{7,6},{0,7},{9,8},{10,9},{11,1... | collective-permute-start | bytes 98312 | tf_op jit(solution)/shard_map/ppermute | solution.py:352

commit v6 on v5

--- a/solution.py
+++ b/solution.py
@@ -1,3 +1,5 @@
+import functools
+
 import jax
 import jax.numpy as jnp
 import numpy as np
@@ -42,7 +44,7 @@
     return np.concatenate([table, table], axis=0)
 
 
-def place_blocks(shape_ref, box_ref, live, base_ref, fast_ref, flag_ref, code_ref):
+def place_blocks(shape_ref, box_ref, live, base_ref, fast_ref, first_ref, many_ref, code_ref):
     lane = lax.broadcasted_iota(jnp.int32, base_ref.shape, 1)
     slot = lax.broadcasted_iota(jnp.int32, base_ref.shape, 0) * 128 + lane
     box = box_ref[...]
@@ -57,22 +59,27 @@
         late = jnp.where(near & ((lane & (BATCH - 1)) >= d), 1, late)
     base_ref[...] = base
     fast_ref[...] = jnp.where(late == 1, DUMP, base)
+    first = jnp.where(late == 1, lane & (BATCH - 1), BATCH)
     for d in (1, 2, 4, 8):
-        late = late | pltpu.roll(late, 128 - d, 1)
-    flag_ref[...] = late
+        first = jnp.minimum(first, pltpu.roll(first, 128 - d, 1))
+        late = late + pltpu.roll(late, 128 - d, 1)
+    first_ref[...] = first
+    many_ref[...] = jnp.where(late > 1, 1, 0)
     code = jnp.where(slot < live, shape_ref[...], 32) * 4 + kind
     code_ref[...] = code.astype(jnp.float32)
 
 
 def spread_kernel(live_ref, q_ref, shape_ref, box_ref, w_any, r_any, out_any, *scratch):
     grid_ref, w_ref, r_ref, pick_ref, half_a, half_b, kind_a, kind_b, tile_a, tile_b, plane_ref = scratch[:11]
-    base_v, fast_v, flag_v, code_ref, base_ref, fast_ref, flag_ref, out_ref, sems, out_sems = scratch[11:]
+    base_v, fast_v, first_v, many_v, code_ref, base_ref, fast_ref, first_ref, many_ref = scratch[11:20]
+    out_ref, sems, out_sems = scratch[20:]
     shapes_n = w_ref.shape[0] // 128
     copies = [pltpu.make_async_copy(w_any, w_ref, sems.at[0]), pltpu.make_async_copy(r_any, r_ref, sems.at[1])]
     for copy in copies:
         copy.start()
-    place_blocks(shape_ref, box_ref, live_ref[0], base_v, fast_v, flag_v, code_ref)
-    for i, (here, there) in enumerate(((base_v, base_ref), (fast_v, fast_ref), (flag_v, flag_ref))):
+    place_blocks(shape_ref, box_ref, live_ref[0], base_v, fast_v, first_v, many_v, code_ref)
+    places = ((base_v, base_ref), (fast_v, fast_ref), (first_v, first_ref), (many_v, many_ref))
+    for i, (here, there) in enumerate(places):
         copies.append(pltpu.make_async_copy(here, there, sems.at[2 + i]))
         copies[-1].start()
     for ref in (half_b, kind_b, tile_a):
@@ -126,22 +133,29 @@
                 grid_ref[pl.ds(r, 3), :] = value
 
     def deposit_rest(step, tile_ref):
-        flag = at(flag_ref, step, 0)
-        for batch in range(1, GROUP // BATCH):
-            flag = flag | at(flag_ref, step, batch * BATCH)
-
-        @pl.when(flag != 0)
+        heads = range(0, GROUP, BATCH)
+        firsts = [at(first_ref, step, i) for i in heads]
+
+        @pl.when(functools.reduce(jnp.minimum, firsts) < BATCH)
+        def _():
+            for i, first in zip(heads, firsts):
+                held = jnp.minimum(first, BATCH - 1)
+                spot = base_ref[step * (GROUP // 128) + i // 128, i % 128 + held]
+                spot = jnp.where(first < BATCH, spot, DUMP)
+                grid_ref[pl.ds(spot, 3), :] += tile_ref[pl.ds((i + held) * 4, 3), :]
+
+        @pl.when(functools.reduce(jnp.maximum, [at(many_ref, step, i) for i in heads]) > 0)
         def _():
             def one_batch(batch, carry):
                 row = step * (GROUP // 128) + batch // (128 // BATCH)
                 head = batch % (128 // BATCH) * BATCH
 
-                @pl.when(flag_ref[row, head] != 0)
+                @pl.when(many_ref[row, head] != 0)
                 def _():
                     def one_block(j, inner):
                         spot = base_ref[row, head + j]
 
-                        @pl.when(fast_ref[row, head + j] != spot)
+                        @pl.when((fast_ref[row, head + j] != spot) & (first_ref[row, head] != j))
                         def _():
                             grid_ref[pl.ds(spot, 3), :] += tile_ref[pl.ds((batch * BATCH + j) * 4, 3), :]
 
@@ -380,12 +394,14 @@
             pltpu.VMEM(rows, jnp.int32),
             pltpu.VMEM(rows, jnp.int32),
             pltpu.VMEM(rows, jnp.int32),
+            pltpu.VMEM(rows, jnp.int32),
             pltpu.VMEM(rows, jnp.float32),
             pltpu.SMEM(rows, jnp.int32),
             pltpu.SMEM(rows, jnp.int32),
             pltpu.SMEM(rows, jnp.int32),
+            pltpu.SMEM(rows, jnp.int32),
             pltpu.VMEM((KZ, SENT, 128), WIRE),
-            pltpu.SemaphoreType.DMA((5,)),
+            pltpu.SemaphoreType.DMA((6,)),
             pltpu.SemaphoreType.DMA((KZ,)),
         ],
         compiler_params=pltpu.CompilerParams(vmem_limit_bytes=56 * 1024 * 1024),

time: 75.4 us -> 74.7 us (level)
  no operation moved by 1% of the time
where the time goes in v6:
time: 74.7 us; the launch traced here: 74.6 us
  blocking collectives  48.8 us (65%)
  Pallas kernels  19.4 us (26%)
  starting transfers between devices  5.71 us (8%)
    all_to_all x1, blocking collectives, on_device(): got = lax.all_to_all(sent, 'bx', split_axis=0, concat_axis=0, tiled=True)  48.8 us
    pallas_call x1, Pallas kernels, on_device(): pl.pallas_call(spread_kernel, out_shape=jax.ShapeDtypeStruct((KZ, SENT, 1...  13 us
    ppermute x2, starting transfers between devices, from_behind(): return lax.ppermute(block, axis, route)  5.71 us
    pallas_call x1, Pallas kernels, on_device(): pl.pallas_call(inner_kernel, out_shape=full, grid=(6,), in_specs=[pl.Bloc...  4.27 us
    pallas_call x1, Pallas kernels, on_device(): pl.pallas_call(outer_kernel, out_shape=full, grid=(2,), in_specs=[pl.Bloc...  1.86 us
  transfers between devices with their start and end apart: 2, of which 0 were waited for; matrix products, arithmetic and copies ran while one was open for 0% of the time, Pallas kernels for 6%

profile of v6, /device:TPU:0, one launch (start us, length us, event | category | flops | bytes accessed | tf_op | source)
XLA Modules:
  0.0 74.6 jit_solution(462194407577431238)
XLA Ops:
  0.7 13.0 %spread.1 = s16[16,608,128]{2,1,0:T(8,128)(2,1)} custom-call(s32[1]{0:T(128)S(6)} %copy.9.live_ref, bf16[2048,128]{1,0:T(8,128)(2,1)} %q_ref.1, s32[16,128]{1,0:T(8,128)} %bitcast.4, s32[16,128]{1,0:T(8,128)} %bitcast.5, bf16[4096,512]{1,0:T(8,128)(2,1)} %bitcast.3, bf16[1024,384]{1,0:T(8,128)(2,1)} %constant.2.clone.r_any), custom_call_target="tpu_custom_call" | custom-call | tf_op jit(solution)/shard_map/spread/pallas_call | solution.py:377
  13.7 48.8 %all_to_all.5.x_ref.refs_0_.refs_1_.refs_2_.refs_3_.refs_4_ = s16[16,608,128]{2,1,0:T(8,128)(2,1)S(1)} all-to-all(s16[16,608,128]{2,1,0:T(8,128)(2,1)} %spread.1), channel_id=1, replica_groups=mesh['bx'=16,'by'=8] {'bx'}, dimensions={0} | all-to-all | bytes 4980736 | tf_op jit(solution)/shard_map/all_to_all | solution.py:417
  62.4 0.3 edge.1
  62.7 2.3 %collective-permute-start = (f32[8,2,512]{2,1,0:T(2,128)S(1)}, f32[8,2,512]{2,1,0:T(2,128)S(1)}, u32[]{:S(2)}, u32[]{:S(2)}) collective-permute-start(f32[8,2,512]{2,1,0:T(2,128)S(1)} %get-tuple-element.7), channel_id=1, source_target_pairs={{7,0},{0,1},{1,2},{2,3},{3,4},{4,5},{5,6},{6,7},{15,8},{8,9},{9,10... | collective-permute-start | bytes 98312 | tf_op jit(solution)/shard_map/ppermute | solution.py:366
  65.0 3.4 %collective-permute-start.1 = (f32[8,2,512]{2,1,0:T(2,128)S(1)}, f32[8,2,512]{2,1,0:T(2,128)S(1)}, u32[]{:S(2)}, u32[]{:S(2)}) collective-permute-start(f32[8,2,512]{2,1,0:T(2,128)S(1)} %get-tuple-element.8), channel_id=1, source_target_pairs={{1,0},{2,1},{3,2},{4,3},{5,4},{6,5},{7,6},{0,7},{9,8},{10,9},{11,1... | collective-permute-start | bytes 98312 | tf_op jit(solution)/shard_map/ppermute | solution.py:366
  68.4 4.3 %inner.1.refs_7_ = f32[8,256,512]{2,1,0:T(8,128)} custom-call(s16[16,608,128]{2,1,0:T(8,128)(2,1)S(1)} %all_to_all.5.x_ref.refs_0_.refs_1_.refs_2_.refs_3_.refs_4_, s16[16,608,128]{2,1,0:T(8,128)(2,1)S(1)} %all_to_all.5.x_ref.refs_0_.refs_1_.refs_2_.refs_3_.refs_4_, s16[16,608,128]{2,1,0:T(8,128)(2,1)S(1)} %all_to_all.5.x_ref.refs_0_.refs_1_.refs_2_.refs_3_.refs_4_, ...), custom_call_target="tpu_custom_call" | custom-call | tf_op jit(solution)/shard_map/inner/pallas_call | solution.py:440
  72.7 0.0 collective-permute-done.refs_5_
  72.7 0.0 collective-permute-done.1.refs_6_
  72.7 1.9 %outer.1 = f32[8,256,512]{2,1,0:T(8,128)} custom-call(s16[16,608,128]{2,1,0:T(8,128)(2,1)S(1)} %all_to_all.5.x_ref.refs_0_.refs_1_.refs_2_.refs_3_.refs_4_, s16[16,608,128]{2,1,0:T(8,128)(2,1)S(1)} %all_to_all.5.x_ref.refs_0_.refs_1_.refs_2_.refs_3_.refs_4_, ...), custom_call_target="tpu_custom_call", output_to_operand_aliasing={{}: (8, {})} | custom-call | tf_op jit(solution)/shard_map/outer/pallas_call | solution.py:450
Async XLA Ops:
  62.7 10.0 %collective-permute-start = (f32[8,2,512]{2,1,0:T(2,128)S(1)}, f32[8,2,512]{2,1,0:T(2,128)S(1)}, u32[]{:S(2)}, u32[]{:S(2)}) collective-permute-start(f32[8,2,512]{2,1,0:T(2,128)S(1)} %get-tuple-element.7), channel_id=1, source_target_pairs={{7,0},{0,1},{1,2},{2,3},{3,4},{4,5},{5,6},{6,7},{15,8},{8,9},{9,10... | collective-permute-start | bytes 98312 | tf_op jit(solution)/shard_map/ppermute | solution.py:366
  65.0 7.7 %collective-permute-start.1 = (f32[8,2,512]{2,1,0:T(2,128)S(1)}, f32[8,2,512]{2,1,0:T(2,128)S(1)}, u32[]{:S(2)}, u32[]{:S(2)}) collective-permute-start(f32[8,2,512]{2,1,0:T(2,128)S(1)} %get-tuple-element.8), channel_id=1, source_target_pairs={{1,0},{2,1},{3,2},{4,3},{5,4},{6,5},{7,6},{0,7},{9,8},{10,9},{11,1... | collective-permute-start | bytes 98312 | tf_op jit(solution)/shard_map/ppermute | solution.py:366

commit v7 on v6

--- a/solution.py
+++ b/solution.py
@@ -10,7 +10,7 @@
 
 NZ = 128
 GROUP = 256
-BATCH = 16
+BATCH = 8
 KZ = 16
 UROWS = 24
 VSLOTS = 34
@@ -30,18 +30,20 @@
 
 def restriction():
     coef = [1.0, 4.0, 6.0, 4.0, 1.0]
-    table = np.zeros((512, 384), np.float32)
+    table = np.zeros((2, 256, 256), np.float32)
     for p in range(8):
         for mm in range(6):
             tap = p + 4 - 2 * mm
             if not 0 <= tap < 5:
                 continue
+            side = p // 4
+            near = mm - 2 * side
             for q in range(8):
                 for r in range(8):
                     z, y = (r - 2) % 8, (q - 2) % 8
-                    lane = z // 4 * 64 + mm % 2 * 32 + z % 4 * 8 + y
-                    table[(p * 8 + q) * 8 + r, mm // 2 * 128 + lane] = coef[tap] / 8.0
-    return np.concatenate([table, table], axis=0)
+                    lane = z // 4 * 64 + near % 2 * 32 + z % 4 * 8 + y
+                    table[side, (p % 4 * 8 + q) * 8 + r, near // 2 * 128 + lane] = coef[tap] / 8.0
+    return np.concatenate([table, table], axis=1).reshape(1024, 256)
 
 
 def place_blocks(shape_ref, box_ref, live, base_ref, fast_ref, first_ref, many_ref, code_ref):
@@ -60,7 +62,7 @@
     base_ref[...] = base
     fast_ref[...] = jnp.where(late == 1, DUMP, base)
     first = jnp.where(late == 1, lane & (BATCH - 1), BATCH)
-    for d in (1, 2, 4, 8):
+    for d in (1, 2, 4):
         first = jnp.minimum(first, pltpu.roll(first, 128 - d, 1))
         late = late + pltpu.roll(late, 128 - d, 1)
     first_ref[...] = first
@@ -82,7 +84,7 @@
     for i, (here, there) in enumerate(places):
         copies.append(pltpu.make_async_copy(here, there, sems.at[2 + i]))
         copies[-1].start()
-    for ref in (half_b, kind_b, tile_a):
+    for ref in (half_b, kind_b):
         ref[...] = jnp.zeros(ref.shape, ref.dtype)
 
     def clear(step, carry):
@@ -106,17 +108,23 @@
             pick = jnp.concatenate([jnp.where(sg == s + i, qg, jnp.zeros_like(qg)) for i in range(2)], axis=1)
             part += jnp.dot(pick, w_ref[s * 128 : (s + 2) * 128, :], preferred_element_type=jnp.float32)
         high = part.astype(jnp.bfloat16)
-        half_ref[:, :512] = high
-        half_ref[:, 512:] = (part - high.astype(jnp.float32)).astype(jnp.bfloat16)
+        low = (part - high.astype(jnp.float32)).astype(jnp.bfloat16)
+        for side in range(2):
+            half_ref[:, side * 512 : side * 512 + 256] = high[:, side * 256 : side * 256 + 256]
+            half_ref[:, side * 512 + 256 : side * 512 + 512] = low[:, side * 256 : side * 256 + 256]
 
     def arrange(half_ref, kind_ref, tile_ref):
-        cells = jnp.dot(half_ref[...], r_ref[...], preferred_element_type=jnp.float32)
+        near, far = [
+            jnp.dot(half_ref[:, c : c + 512], r_ref[c : c + 512, :], preferred_element_type=jnp.float32)
+            for c in (0, 512)
+        ]
+        cells = [near[:, :128], near[:, 128:] + far[:, :128], far[:, 128:]]
         kind = kind_ref[...]
         z_odd = kind >= 2.0
         y_odd = (kind == 1.0) | (kind == 3.0)
         y_upper = (lax.broadcasted_iota(jnp.int32, kind.shape, 1) & 4) != 0
         for du in range(3):
-            rows = cells[:, du * 128 : (du + 1) * 128]
+            rows = cells[du]
             rows = jnp.where(z_odd, pltpu.roll(rows, 64, 1), rows)
             crossed = jnp.where(y_upper, pltpu.roll(rows, 4, 1), pltpu.roll(rows, 124, 1))
             tile_ref[pl.ds(du, GROUP, stride=4), :] = jnp.where(y_odd, crossed, rows)
@@ -171,10 +179,10 @@
         step = 2 * pair
         arrange(half_b, kind_b, tile_b)
         product(step, half_a, kind_a)
-        deposit(jnp.maximum(step - 2, 0), tile_a)
+        deposit(jnp.maximum(step - 1, 0), tile_b)
         arrange(half_a, kind_a, tile_a)
         product(step + 1, half_b, kind_b)
-        deposit(jnp.maximum(step - 1, 0), tile_b)
+        deposit(step, tile_a)
 
         @pl.when(pair > 0)
         def _():
@@ -186,7 +194,6 @@
     pairs = (live_ref[0] + 2 * GROUP - 1) // (2 * GROUP)
     lax.fori_loop(0, pairs, two_groups, 0)
     arrange(half_b, kind_b, tile_b)
-    deposit(2 * pairs - 2, tile_a)
     deposit(2 * pairs - 1, tile_b)
     deposit_rest(2 * pairs - 1, tile_b)
 
@@ -382,7 +389,7 @@
         scratch_shapes=[
             pltpu.VMEM((GROWS + SPARE, 128), jnp.float32),
             pltpu.VMEM((shapes_n * atoms, cells), jnp.bfloat16),
-            pltpu.VMEM((1024, 384), jnp.bfloat16),
+            pltpu.VMEM((1024, 256), jnp.bfloat16),
             pltpu.VMEM((GROUP, shapes_n * atoms), jnp.bfloat16),
             pltpu.VMEM((GROUP, 1024), jnp.bfloat16),
             pltpu.VMEM((GROUP, 1024), jnp.bfloat16),

time: 74.7 us -> 73.3 us (0.981)
  blocking collectives: 48.8 us -> 48 us
    all_to_all x1, blocking collectives: 48.8 us -> 48 us  [on_device(): got = lax.all_to_all(sent, 'bx', split_axis=0, concat_axis=0, tiled=True)]
where the time goes in v7:
time: 73.3 us
  blocking collectives  48 us (65%)
  Pallas kernels  18.9 us (26%)
  starting transfers between devices  5.71 us (8%)
    all_to_all x1, blocking collectives, on_device(): got = lax.all_to_all(sent, 'bx', split_axis=0, concat_axis=0, tiled=True)  48 us
    pallas_call x1, Pallas kernels, on_device(): pl.pallas_call(spread_kernel, out_shape=jax.ShapeDtypeStruct((KZ, SENT, 1...  12.5 us
    ppermute x2, starting transfers between devices, from_behind(): return lax.ppermute(block, axis, route)  5.71 us
    pallas_call x1, Pallas kernels, on_device(): pl.pallas_call(inner_kernel, out_shape=full, grid=(6,), in_specs=[pl.Bloc...  4.27 us
    pallas_call x1, Pallas kernels, on_device(): pl.pallas_call(outer_kernel, out_shape=full, grid=(2,), in_specs=[pl.Bloc...  1.86 us
  transfers between devices with their start and end apart: 2, of which 0 were waited for; matrix products, arithmetic and copies ran while one was open for 0% of the time, Pallas kernels for 6%

profile of v7, /device:TPU:0, one launch (start us, length us, event | category | flops | bytes accessed | tf_op | source)
XLA Modules:
  0.0 73.3 jit_solution(13302422235972741593)
XLA Ops:
  0.7 12.5 %spread.1 = s16[16,608,128]{2,1,0:T(8,128)(2,1)} custom-call(s32[1]{0:T(128)S(6)} %copy.9.live_ref, bf16[2048,128]{1,0:T(8,128)(2,1)} %q_ref.1, s32[16,128]{1,0:T(8,128)} %bitcast.4, s32[16,128]{1,0:T(8,128)} %bitcast.5, bf16[4096,512]{1,0:T(8,128)(2,1)} %bitcast.3, bf16[1024,256]{1,0:T(8,128)(2,1)} %constant.2.clone.r_any), custom_call_target="tpu_custom_call" | custom-call | tf_op jit(solution)/shard_map/spread/pallas_call | solution.py:384
  13.2 48.0 %all_to_all.5.x_ref.refs_0_.refs_1_.refs_2_.refs_3_.refs_4_ = s16[16,608,128]{2,1,0:T(8,128)(2,1)S(1)} all-to-all(s16[16,608,128]{2,1,0:T(8,128)(2,1)} %spread.1), channel_id=1, replica_groups=mesh['bx'=16,'by'=8] {'bx'}, dimensions={0} | all-to-all | bytes 4980736 | tf_op jit(solution)/shard_map/all_to_all | solution.py:424
  61.2 0.3 edge.1
  61.5 3.4 %collective-permute-start = (f32[8,2,512]{2,1,0:T(2,128)S(1)}, f32[8,2,512]{2,1,0:T(2,128)S(1)}, u32[]{:S(2)}, u32[]{:S(2)}) collective-permute-start(f32[8,2,512]{2,1,0:T(2,128)S(1)} %get-tuple-element.7), channel_id=1, source_target_pairs={{7,0},{0,1},{1,2},{2,3},{3,4},{4,5},{5,6},{6,7},{15,8},{8,9},{9,10... | collective-permute-start | bytes 98312 | tf_op jit(solution)/shard_map/ppermute | solution.py:373
  64.8 2.4 %collective-permute-start.1 = (f32[8,2,512]{2,1,0:T(2,128)S(1)}, f32[8,2,512]{2,1,0:T(2,128)S(1)}, u32[]{:S(2)}, u32[]{:S(2)}) collective-permute-start(f32[8,2,512]{2,1,0:T(2,128)S(1)} %get-tuple-element.8), channel_id=1, source_target_pairs={{1,0},{2,1},{3,2},{4,3},{5,4},{6,5},{7,6},{0,7},{9,8},{10,9},{11,1... | collective-permute-start | bytes 98312 | tf_op jit(solution)/shard_map/ppermute | solution.py:373
  67.2 4.3 %inner.1.refs_7_ = f32[8,256,512]{2,1,0:T(8,128)} custom-call(s16[16,608,128]{2,1,0:T(8,128)(2,1)S(1)} %all_to_all.5.x_ref.refs_0_.refs_1_.refs_2_.refs_3_.refs_4_, s16[16,608,128]{2,1,0:T(8,128)(2,1)S(1)} %all_to_all.5.x_ref.refs_0_.refs_1_.refs_2_.refs_3_.refs_4_, s16[16,608,128]{2,1,0:T(8,128)(2,1)S(1)} %all_to_all.5.x_ref.refs_0_.refs_1_.refs_2_.refs_3_.refs_4_, ...), custom_call_target="tpu_custom_call" | custom-call | tf_op jit(solution)/shard_map/inner/pallas_call | solution.py:447
  71.4 0.0 collective-permute-done.refs_5_
  71.5 0.0 collective-permute-done.1.refs_6_
  71.5 1.9 %outer.1 = f32[8,256,512]{2,1,0:T(8,128)} custom-call(s16[16,608,128]{2,1,0:T(8,128)(2,1)S(1)} %all_to_all.5.x_ref.refs_0_.refs_1_.refs_2_.refs_3_.refs_4_, s16[16,608,128]{2,1,0:T(8,128)(2,1)S(1)} %all_to_all.5.x_ref.refs_0_.refs_1_.refs_2_.refs_3_.refs_4_, ...), custom_call_target="tpu_custom_call", output_to_operand_aliasing={{}: (8, {})} | custom-call | tf_op jit(solution)/shard_map/outer/pallas_call | solution.py:457
Async XLA Ops:
  61.5 10.0 %collective-permute-start = (f32[8,2,512]{2,1,0:T(2,128)S(1)}, f32[8,2,512]{2,1,0:T(2,128)S(1)}, u32[]{:S(2)}, u32[]{:S(2)}) collective-permute-start(f32[8,2,512]{2,1,0:T(2,128)S(1)} %get-tuple-element.7), channel_id=1, source_target_pairs={{7,0},{0,1},{1,2},{2,3},{3,4},{4,5},{5,6},{6,7},{15,8},{8,9},{9,10... | collective-permute-start | bytes 98312 | tf_op jit(solution)/shard_map/ppermute | solution.py:373
  64.8 6.6 %collective-permute-start.1 = (f32[8,2,512]{2,1,0:T(2,128)S(1)}, f32[8,2,512]{2,1,0:T(2,128)S(1)}, u32[]{:S(2)}, u32[]{:S(2)}) collective-permute-start(f32[8,2,512]{2,1,0:T(2,128)S(1)} %get-tuple-element.8), channel_id=1, source_target_pairs={{1,0},{2,1},{3,2},{4,3},{5,4},{6,5},{7,6},{0,7},{9,8},{10,9},{11,1... | collective-permute-start | bytes 98312 | tf_op jit(solution)/shard_map/ppermute | solution.py:373

commit v8 on v7

--- a/solution.py
+++ b/solution.py
@@ -281,9 +281,9 @@
     out_ref[begin : begin + 16, :] = jnp.concatenate([marked, rest], axis=0).astype(jnp.int32).astype(out_ref.dtype)
 
 
-def take_tails(tails, tail_ref, grow_ref):
+def take_tails(x_ref, tail_ref, grow_ref):
     for src in range(16):
-        tail = jnp.concatenate([t[src] for t in tails], axis=0).astype(jnp.float32)
+        tail = x_ref[src, TAIL:SENT, :].astype(jnp.float32)
         grow = jnp.exp2(tail[SCALE_ROW - TAIL : SCALE_ROW - TAIL + 1] * 0.0625) / LEVELS
         grow_ref[src * 8 : src * 8 + 8, :] = jnp.broadcast_to(grow, (8, 128))
         tail_ref[src * 80 : (src + 1) * 80, :] = tail * grow
@@ -317,9 +317,9 @@
 
 
 def edge_kernel(x_ref, *refs):
-    tails, (down_ref, up_ref), scratch = refs[:5], refs[5:7], refs[7:]
-    take_tails(tails, *scratch[:2])
-    blocks = turn(lambda src, which: x_ref[src], (32,), *scratch[:2], scratch[2].at[0])
+    (down_ref, up_ref), scratch = refs[:2], refs[2:]
+    take_tails(x_ref, *scratch[:2])
+    blocks = turn(lambda src, which: x_ref[src, EDGE:TAIL, :], (32,), *scratch[:2], scratch[2].at[0])
     for c, block in enumerate(blocks):
         down_ref[:, :, c * 128 : (c + 1) * 128] = block[0][:, 6:8]
         up_ref[:, :, c * 128 : (c + 1) * 128] = block[0][:, 0:2]
@@ -328,7 +328,7 @@
 def assemble(x_ref, first, out_ref, scratch):
     tail_ref, grow_ref, turn_refs = scratch
     for pair in range(2):
-        rows_of = lambda src, which: x_ref[src, (2 * pair + which) * 16 : (2 * pair + which + 1) * 16, :]
+        rows_of = lambda src, which: x_ref[src, pl.ds(pl.multiple_of((first + 2 * pair + which) * 16, 16), 16), :]
         slabs = (first + 2 * pair, first + 2 * pair + 1)
         blocks = turn(rows_of, slabs, tail_ref, grow_ref, turn_refs.at[pair])
         for c, block in enumerate(blocks):
@@ -338,23 +338,23 @@
 
 
 def inner_kernel(x_ref, *refs):
-    tails, out_ref, scratch = refs[:5], refs[5], refs[6:]
+    out_ref, scratch = refs[0], refs[1:]
     step = pl.program_id(0)
 
     @pl.when(step == 0)
     def _():
-        take_tails(tails, *scratch[:2])
+        take_tails(x_ref, *scratch[:2])
 
     assemble(x_ref, 4 * step + 4, out_ref, scratch)
 
 
 def outer_kernel(x_ref, *refs):
-    tails, (below_ref, above_ref, _, out_ref), scratch = refs[:5], refs[5:9], refs[9:]
+    (below_ref, above_ref, _, out_ref), scratch = refs[:4], refs[4:]
     step = pl.program_id(0)
 
     @pl.when(step == 0)
     def _():
-        take_tails(tails, *scratch[:2])
+        take_tails(x_ref, *scratch[:2])
 
     assemble(x_ref, 28 * step, out_ref, scratch)
 
@@ -422,8 +422,6 @@
         jnp.asarray(restriction(), jnp.bfloat16),
     )
     got = lax.all_to_all(sent, "bx", split_axis=0, concat_axis=0, tiled=True)
-    piece = lambda i: pl.BlockSpec((KZ, 16, 128), lambda p: (0, i, 0))
-    tails = [piece(TAIL // 16 + i) for i in range(5)]
     small = pl.BlockSpec((8, 2, 512), lambda p: (0, 0, 0))
     full = jax.ShapeDtypeStruct((8, 256, 512), jnp.float32)
     scratch = [
@@ -436,37 +434,35 @@
         edge_kernel,
         out_shape=(jax.ShapeDtypeStruct((8, 2, 512), jnp.float32),) * 2,
         grid=(1,),
-        in_specs=[piece(EDGE // 16)] + tails,
+        in_specs=[vmem],
         out_specs=(small, small),
         scratch_shapes=scratch,
         compiler_params=params,
         name="edge",
-    )(*[got] * 6)
+    )(got)
     below = from_behind(up, "by", 1)
     above = from_behind(down, "by", -1)
     inner = pl.pallas_call(
         inner_kernel,
         out_shape=full,
         grid=(6,),
-        in_specs=[pl.BlockSpec((KZ, 64, 128), lambda p: (0, p + 1, 0))] + tails,
+        in_specs=[vmem],
         out_specs=pl.BlockSpec((8, 32, 512), lambda p: (0, p + 1, 0)),
         scratch_shapes=scratch,
         compiler_params=params,
         name="inner",
-    )(*[got] * 6)
+    )(got)
     return pl.pallas_call(
         outer_kernel,
         out_shape=full,
         grid=(2,),
-        in_specs=[pl.BlockSpec((KZ, 64, 128), lambda p: (0, 7 * p, 0))]
-        + tails
-        + [small, small, pl.BlockSpec(memory_space=pl.ANY)],
+        in_specs=[vmem, small, small, hbm],
         out_specs=pl.BlockSpec((8, 32, 512), lambda p: (0, 7 * p, 0)),
         scratch_shapes=scratch,
-        input_output_aliases={8: 0},
+        input_output_aliases={3: 0},
         compiler_params=params,
         name="outer",
-    )(*[got] * 6, below, above, inner)
+    )(got, below, above, inner)
 
 
 def solution(mesh):

time: 73.3 us -> 72.7 us (level)
  blocking collectives: 48 us -> 46.8 us
    all_to_all x1, blocking collectives: 48 us -> 46.8 us  [on_device(): got = lax.all_to_all(sent, 'bx', split_axis=0, concat_axis=0, tiled=True)]
  transfers between devices with their start and end apart: 2 -> 2, of which waited for: 0 -> 0; matrix products, arithmetic and copies ran while one was open for 0% -> 0% of each run, Pallas kernels for 6% -> 5%
where the time goes in v8:
time: 72.7 us; the launch traced here: 72.1 us
  blocking collectives  46.8 us (64%)
  Pallas kernels  18.6 us (26%)
  starting transfers between devices  6.05 us (8%)
    all_to_all x1, blocking collectives, on_device(): got = lax.all_to_all(sent, 'bx', split_axis=0, concat_axis=0, tiled=True)  46.8 us
    pallas_call x1, Pallas kernels, on_device(): pl.pallas_call(spread_kernel, out_shape=jax.ShapeDtypeStruct((KZ, SENT, 1...  12.7 us
    ppermute x2, starting transfers between devices, from_behind(): return lax.ppermute(block, axis, route)  6.05 us
    pallas_call x1, Pallas kernels, on_device(): pl.pallas_call(inner_kernel, out_shape=full, grid=(6,), in_specs=[vmem],...  3.95 us
    pallas_call x1, Pallas kernels, on_device(): pl.pallas_call(outer_kernel, out_shape=full, grid=(2,), in_specs=[vmem, s...  1.68 us
  transfers between devices with their start and end apart: 2, of which 0 were waited for; matrix products, arithmetic and copies ran while one was open for 0% of the time, Pallas kernels for 5%

profile of v8, /device:TPU:0, one launch (start us, length us, event | category | flops | bytes accessed | tf_op | source)
XLA Modules:
  0.0 72.1 jit_solution(11178704129506947891)
XLA Ops:
  0.7 12.7 %spread.1 = s16[16,608,128]{2,1,0:T(8,128)(2,1)} custom-call(s32[1]{0:T(128)S(6)} %copy.9.live_ref, bf16[2048,128]{1,0:T(8,128)(2,1)} %q_ref.1, s32[16,128]{1,0:T(8,128)} %bitcast.4, s32[16,128]{1,0:T(8,128)} %bitcast.5, bf16[4096,512]{1,0:T(8,128)(2,1)} %bitcast.3, bf16[1024,256]{1,0:T(8,128)(2,1)} %constant.2.clone.r_any), custom_call_target="tpu_custom_call" | custom-call | tf_op jit(solution)/shard_map/spread/pallas_call | solution.py:384
  13.3 46.8 %all_to_all.5.x_ref = s16[16,608,128]{2,1,0:T(8,128)(2,1)S(1)} all-to-all(s16[16,608,128]{2,1,0:T(8,128)(2,1)} %spread.1), channel_id=1, replica_groups=mesh['bx'=16,'by'=8] {'bx'}, dimensions={0} | all-to-all | bytes 4980736 | tf_op jit(solution)/shard_map/all_to_all | solution.py:424
  60.2 0.3 edge.1
  60.4 4.2 %collective-permute-start = (f32[8,2,512]{2,1,0:T(2,128)S(1)}, f32[8,2,512]{2,1,0:T(2,128)S(1)}, u32[]{:S(2)}, u32[]{:S(2)}) collective-permute-start(f32[8,2,512]{2,1,0:T(2,128)S(1)} %get-tuple-element.7), channel_id=1, source_target_pairs={{7,0},{0,1},{1,2},{2,3},{3,4},{4,5},{5,6},{6,7},{15,8},{8,9},{9,10... | collective-permute-start | bytes 98312 | tf_op jit(solution)/shard_map/ppermute | solution.py:373
  64.6 1.9 %collective-permute-start.1 = (f32[8,2,512]{2,1,0:T(2,128)S(1)}, f32[8,2,512]{2,1,0:T(2,128)S(1)}, u32[]{:S(2)}, u32[]{:S(2)}) collective-permute-start(f32[8,2,512]{2,1,0:T(2,128)S(1)} %get-tuple-element.8), channel_id=1, source_target_pairs={{1,0},{2,1},{3,2},{4,3},{5,4},{6,5},{7,6},{0,7},{9,8},{10,9},{11,1... | collective-permute-start | bytes 98312 | tf_op jit(solution)/shard_map/ppermute | solution.py:373
  66.5 3.9 %inner.1.refs_2_ = f32[8,256,512]{2,1,0:T(8,128)} custom-call(s16[16,608,128]{2,1,0:T(8,128)(2,1)S(1)} %all_to_all.5.x_ref), custom_call_target="tpu_custom_call" | custom-call | tf_op jit(solution)/shard_map/inner/pallas_call | solution.py:445
  70.4 0.0 collective-permute-done.refs_0_
  70.4 0.0 collective-permute-done.1.refs_1_
  70.5 1.7 %outer.1 = f32[8,256,512]{2,1,0:T(8,128)} custom-call(s16[16,608,128]{2,1,0:T(8,128)(2,1)S(1)} %all_to_all.5.x_ref, f32[8,2,512]{2,1,0:T(2,128)S(1)} %collective-permute-done.refs_0_, f32[8,2,512]{2,1,0:T(2,128)S(1)} %collective-permute-done.1.refs_1_, f32[8,256,512]{2,1,0:T(8,128)} %inner.1.refs_2_), custom_call_target="tpu_custom_call", output_to_operand_aliasing={{}: (3, {})} | custom-call | tf_op jit(solution)/shard_map/outer/pallas_call | solution.py:455
Async XLA Ops:
  60.4 10.0 %collective-permute-start = (f32[8,2,512]{2,1,0:T(2,128)S(1)}, f32[8,2,512]{2,1,0:T(2,128)S(1)}, u32[]{:S(2)}, u32[]{:S(2)}) collective-permute-start(f32[8,2,512]{2,1,0:T(2,128)S(1)} %get-tuple-element.7), channel_id=1, source_target_pairs={{7,0},{0,1},{1,2},{2,3},{3,4},{4,5},{5,6},{6,7},{15,8},{8,9},{9,10... | collective-permute-start | bytes 98312 | tf_op jit(solution)/shard_map/ppermute | solution.py:373
  64.6 5.8 %collective-permute-start.1 = (f32[8,2,512]{2,1,0:T(2,128)S(1)}, f32[8,2,512]{2,1,0:T(2,128)S(1)}, u32[]{:S(2)}, u32[]{:S(2)}) collective-permute-start(f32[8,2,512]{2,1,0:T(2,128)S(1)} %get-tuple-element.8), channel_id=1, source_target_pairs={{1,0},{2,1},{3,2},{4,3},{5,4},{6,5},{7,6},{0,7},{9,8},{10,9},{11,1... | collective-permute-start | bytes 98312 | tf_op jit(solution)/shard_map/ppermute | solution.py:373

commit v9 on v8

--- a/solution.py
+++ b/solution.py
@@ -327,7 +327,7 @@
 
 def assemble(x_ref, first, out_ref, scratch):
     tail_ref, grow_ref, turn_refs = scratch
-    for pair in range(2):
+    for pair in range(4):
         rows_of = lambda src, which: x_ref[src, pl.ds(pl.multiple_of((first + 2 * pair + which) * 16, 16), 16), :]
         slabs = (first + 2 * pair, first + 2 * pair + 1)
         blocks = turn(rows_of, slabs, tail_ref, grow_ref, turn_refs.at[pair])
@@ -345,7 +345,7 @@
     def _():
         take_tails(x_ref, *scratch[:2])
 
-    assemble(x_ref, 4 * step + 4, out_ref, scratch)
+    assemble(x_ref, 8 * step + 8, out_ref, scratch)
 
 
 def outer_kernel(x_ref, *refs):
@@ -356,7 +356,7 @@
     def _():
         take_tails(x_ref, *scratch[:2])
 
-    assemble(x_ref, 28 * step, out_ref, scratch)
+    assemble(x_ref, 24 * step, out_ref, scratch)
 
     @pl.when(step == 0)
     def _():
@@ -364,7 +364,7 @@
 
     @pl.when(step == 1)
     def _():
-        out_ref[:, 30:32, :] += above_ref[...]
+        out_ref[:, 62:64, :] += above_ref[...]
 
 
 def from_behind(block, axis, distance):
@@ -427,7 +427,7 @@
     scratch = [
         pltpu.VMEM((16 * 80, 128), jnp.float32),
         pltpu.VMEM((128, 128), jnp.float32),
-        pltpu.VMEM((2, 512, 128), jnp.float32),
+        pltpu.VMEM((4, 512, 128), jnp.float32),
     ]
     params = pltpu.CompilerParams(vmem_limit_bytes=40 * 1024 * 1024)
     down, up = pl.pallas_call(
@@ -445,9 +445,9 @@
     inner = pl.pallas_call(
         inner_kernel,
         out_shape=full,
-        grid=(6,),
+        grid=(2,),
         in_specs=[vmem],
-        out_specs=pl.BlockSpec((8, 32, 512), lambda p: (0, p + 1, 0)),
+        out_specs=pl.BlockSpec((8, 64, 512), lambda p: (0, p + 1, 0)),
         scratch_shapes=scratch,
         compiler_params=params,
         name="inner",
@@ -457,7 +457,7 @@
         out_shape=full,
         grid=(2,),
         in_specs=[vmem, small, small, hbm],
-        out_specs=pl.BlockSpec((8, 32, 512), lambda p: (0, 7 * p, 0)),
+        out_specs=pl.BlockSpec((8, 64, 512), lambda p: (0, 3 * p, 0)),
         scratch_shapes=scratch,
         input_output_aliases={3: 0},
         compiler_params=params,

time: 72.7 us -> 72.8 us (level)
  blocking collectives: 46.8 us -> 43.1 us
  Pallas kernels: 18.6 us -> 20.9 us
  starting transfers between devices: 6.05 us -> 7.15 us
    all_to_all x1, blocking collectives: 46.8 us -> 43.1 us  [on_device(): got = lax.all_to_all(sent, 'bx', split_axis=0, concat_axis=0, tiled=True)]
    pallas_call x1, Pallas kernels: 12.7 us -> 15.8 us  [on_device(): pl.pallas_call(spread_kernel, out_shape=jax.ShapeDtypeStruct((KZ, SENT, 1...]
    pallas_call x1, Pallas kernels: 3.95 us -> 2.36 us  [on_device(): pl.pallas_call(inner_kernel, out_shape=full, grid=(2,), in_specs=[vmem],...]
    ppermute x2, starting transfers between devices: 6.05 us -> 7.15 us  [from_behind(): return lax.ppermute(block, axis, route)]
  transfers between devices with their start and end apart: 2 -> 2, of which waited for: 0 -> 1; matrix products, arithmetic and copies ran while one was open for 0% -> 0% of each run, Pallas kernels for 5% -> 3%
where the time goes in v9:
time: 72.8 us; the launch traced here: 72.1 us
  blocking collectives  43.1 us (59%)
  Pallas kernels  20.9 us (29%)
  starting transfers between devices  7.15 us (10%)
    all_to_all x1, blocking collectives, on_device(): got = lax.all_to_all(sent, 'bx', split_axis=0, concat_axis=0, tiled=True)  43.1 us
    pallas_call x1, Pallas kernels, on_device(): pl.pallas_call(spread_kernel, out_shape=jax.ShapeDtypeStruct((KZ, SENT, 1...  15.8 us
    ppermute x2, starting transfers between devices, from_behind(): return lax.ppermute(block, axis, route)  7.15 us
    pallas_call x1, Pallas kernels, on_device(): pl.pallas_call(outer_kernel, out_shape=full, grid=(2,), in_specs=[vmem, s...  2.39 us
    pallas_call x1, Pallas kernels, on_device(): pl.pallas_call(inner_kernel, out_shape=full, grid=(2,), in_specs=[vmem],...  2.36 us
  transfers between devices with their start and end apart: 2, of which 1 were waited for; matrix products, arithmetic and copies ran while one was open for 0% of the time, Pallas kernels for 3%

profile of v9, /device:TPU:0, one launch (start us, length us, event | category | flops | bytes accessed | tf_op | source)
XLA Modules:
  0.0 72.1 jit_solution(18011268221039904955)
XLA Ops:
  0.7 15.8 %spread.1 = s16[16,608,128]{2,1,0:T(8,128)(2,1)} custom-call(s32[1]{0:T(128)S(6)} %copy.9.live_ref, bf16[2048,128]{1,0:T(8,128)(2,1)} %q_ref.1, s32[16,128]{1,0:T(8,128)} %bitcast.4, s32[16,128]{1,0:T(8,128)} %bitcast.5, bf16[4096,512]{1,0:T(8,128)(2,1)} %bitcast.3, bf16[1024,256]{1,0:T(8,128)(2,1)} %constant.2.clone.r_any), custom_call_target="tpu_custom_call" | custom-call | tf_op jit(solution)/shard_map/spread/pallas_call | solution.py:384
  16.5 43.1 %all_to_all.5.x_ref = s16[16,608,128]{2,1,0:T(8,128)(2,1)S(1)} all-to-all(s16[16,608,128]{2,1,0:T(8,128)(2,1)} %spread.1), channel_id=1, replica_groups=mesh['bx'=16,'by'=8] {'bx'}, dimensions={0} | all-to-all | bytes 4980736 | tf_op jit(solution)/shard_map/all_to_all | solution.py:424
  59.7 0.3 edge.1
  59.9 4.3 %collective-permute-start = (f32[8,2,512]{2,1,0:T(2,128)S(1)}, f32[8,2,512]{2,1,0:T(2,128)S(1)}, u32[]{:S(2)}, u32[]{:S(2)}) collective-permute-start(f32[8,2,512]{2,1,0:T(2,128)S(1)} %get-tuple-element.7), channel_id=1, source_target_pairs={{7,0},{0,1},{1,2},{2,3},{3,4},{4,5},{5,6},{6,7},{15,8},{8,9},{9,10... | collective-permute-start | bytes 98312 | tf_op jit(solution)/shard_map/ppermute | solution.py:373
  64.3 2.8 %collective-permute-start.1 = (f32[8,2,512]{2,1,0:T(2,128)S(1)}, f32[8,2,512]{2,1,0:T(2,128)S(1)}, u32[]{:S(2)}, u32[]{:S(2)}) collective-permute-start(f32[8,2,512]{2,1,0:T(2,128)S(1)} %get-tuple-element.8), channel_id=1, source_target_pairs={{1,0},{2,1},{3,2},{4,3},{5,4},{6,5},{7,6},{0,7},{9,8},{10,9},{11,1... | collective-permute-start | bytes 98312 | tf_op jit(solution)/shard_map/ppermute | solution.py:373
  67.1 2.4 %inner.1.refs_2_ = f32[8,256,512]{2,1,0:T(8,128)} custom-call(s16[16,608,128]{2,1,0:T(8,128)(2,1)S(1)} %all_to_all.5.x_ref), custom_call_target="tpu_custom_call" | custom-call | tf_op jit(solution)/shard_map/inner/pallas_call | solution.py:445
  69.4 0.0 collective-permute-done.refs_0_
  69.4 0.2 collective-permute-done.1.refs_1_
  69.7 2.4 %outer.1 = f32[8,256,512]{2,1,0:T(8,128)} custom-call(s16[16,608,128]{2,1,0:T(8,128)(2,1)S(1)} %all_to_all.5.x_ref, f32[8,2,512]{2,1,0:T(2,128)S(1)} %collective-permute-done.refs_0_, f32[8,2,512]{2,1,0:T(2,128)S(1)} %collective-permute-done.1.refs_1_, f32[8,256,512]{2,1,0:T(8,128)} %inner.1.refs_2_), custom_call_target="tpu_custom_call", output_to_operand_aliasing={{}: (3, {})} | custom-call | tf_op jit(solution)/shard_map/outer/pallas_call | solution.py:455
Async XLA Ops:
  59.9 9.5 %collective-permute-start = (f32[8,2,512]{2,1,0:T(2,128)S(1)}, f32[8,2,512]{2,1,0:T(2,128)S(1)}, u32[]{:S(2)}, u32[]{:S(2)}) collective-permute-start(f32[8,2,512]{2,1,0:T(2,128)S(1)} %get-tuple-element.7), channel_id=1, source_target_pairs={{7,0},{0,1},{1,2},{2,3},{3,4},{4,5},{5,6},{6,7},{15,8},{8,9},{9,10... | collective-permute-start | bytes 98312 | tf_op jit(solution)/shard_map/ppermute | solution.py:373
  64.3 5.4 %collective-permute-start.1 = (f32[8,2,512]{2,1,0:T(2,128)S(1)}, f32[8,2,512]{2,1,0:T(2,128)S(1)}, u32[]{:S(2)}, u32[]{:S(2)}) collective-permute-start(f32[8,2,512]{2,1,0:T(2,128)S(1)} %get-tuple-element.8), channel_id=1, source_target_pairs={{1,0},{2,1},{3,2},{4,3},{5,4},{6,5},{7,6},{0,7},{9,8},{10,9},{11,1... | collective-permute-start | bytes 98312 | tf_op jit(solution)/shard_map/ppermute | solution.py:373
